TPU v7x, 32 devices: a whole 2x2x4 slice. The times are simulated.
32 devices in a mesh: freq: 4 (over x, core), tile: 8 (over z, y).
Axes of the slice: x: 2, y: 2, z: 4, core: 2. Of those that a mesh axis runs over, the one named last changes fastest.
Arguments:
- visibilities: bfloat16 [8, 8, 64, 4096], P('tile', None, None, 'freq'), may hold values from -6 to 6
- uv_rows: float32 [8, 2, 4096], P('tile', None, 'freq'), may hold values from -5.76 to 5.76
- chan_scale: float32 [64], replicated, may hold values from 0.7 to 1.4
- valid_rows: int32 [8, 4], P('tile', 'freq'), may hold values from 512 to 1024
- aterm: float32 [4, 512, 2, 1024], P('freq'), may hold values from -4 to 4
- taper: float32 [32, 32], replicated, may hold values from 0.25 to 1.75
- stations: int32 [8, 4, 32, 2], P('tile', 'freq'), may hold values from 0 to 511, all different within a row
- owner: int32 [8, 4, 32, 1], P('tile', 'freq'), may hold values from 0 to 31; in each aligned block of 32 rows (0 to 31, 32 to 63, ..., all dimensions but the last counted through in order) at most 2 rows name the same one
- u_offset: int32 [8, 4, 32, 1], P('tile', 'freq'), may hold values from 0 to 255
- v_start: int32 [8, 4, 32, 1], P('tile', 'freq'), may hold values from 0 to 224
Outputs:
- uv_band: float32 [8, 8192, 256], P(None, ('freq', 'tile'))
Inputs may be any that keep to these rules, and one draw needn't show every extreme that they name: `owner`: among the 32 subgrids of one index of tile and one of freq, no tile is named more than 2 times; in every draw some tile is named exactly 2 times by some of them. The two stations of a subgrid differ.
All inputs are finite; a program needn't handle non-finite values.
Results may differ from a plain program's by a relative error of at most 0.0047.
Values may be sent and summed in bfloat16 or wider, within the bound.
No kernel may reach another device: no remote copies, remote signals or barrier semaphores. Data moves between devices by JAX's collectives and lax.ppermute only.
A program may use at most 128 MiB of HBM per device.

v0:
```python
import functools
import math

import jax
import jax.numpy as jnp
import ml_dtypes
import numpy as np
from jax import lax
from jax.experimental import pallas as pl
from jax.experimental.pallas import tpu as pltpu
from jax.sharding import PartitionSpec as P

SG = 32
HALF = SG // 2
TSTEP = 128
CHAN_G = 16
FAN = CHAN_G * TSTEP
TILE_W = 256
BAND_V = 256
LANES = 128
COMPS = 8
POL = 4
POS_ROWS = 8
NO_PLACE = 512.0
CAP = 2
U_STEP = SG + 3
V_STEP = 2 * SG + 1
W_STEP = CHAN_G + 1
VMEM_LIMIT = 60 << 20
f32 = jnp.float32
bf16 = jnp.bfloat16


def vmem():
    return pl.BlockSpec(memory_space=pltpu.VMEM)


def smem():
    return pl.BlockSpec(memory_space=pltpu.SMEM)


IMAGE_ROWS = np.array([HALF + i for i in range(HALF)] + [0] + [HALF - i for i in range(1, HALF)])


def split(matrix):
    high = matrix.astype(np.float32).astype(ml_dtypes.bfloat16)
    low = (matrix - high.astype(np.float64)).astype(np.float32).astype(ml_dtypes.bfloat16)
    return high, low


def fourier():
    cells = np.arange(SG) - HALF
    angles = (cells[:, None] * cells[None, :] % SG) * (2.0 * math.pi / SG)
    return np.cos(angles), -np.sin(angles)


def lane_transform():
    cos, sin = fourier()
    table = np.zeros((2, 2, 2, SG, 2, 2, 2, SG))
    for p in range(2):
        y_re = {(0, 0): cos, (1, 1): -cos, (1, 0): -sin, (0, 1): -sin}
        y_im = {(0, 0): sin, (1, 1): -sin, (1, 0): cos, (0, 1): cos}
        for gain in range(2):
            for part in range(2):
                re, im = y_re[gain, part].T, y_im[gain, part].T
                table[gain, p, part, :, 0, p, 0, :] = re
                table[gain, p, part, :, 0, p, 1, :] = im
                table[gain, p, part, :, 1, p, 0, :] = -im
                table[gain, p, part, :, 1, p, 1, :] = re
    return split(table.reshape(256, 256))


def row_transform():
    cos, sin = fourier()
    high, low = split(np.concatenate([cos[:, IMAGE_ROWS], sin[:, IMAGE_ROWS]], 1))
    return np.concatenate([high, high, low], 1)


def lane_tiles():
    table = np.zeros((POL, SG, POL, POL, SG))
    for q in range(POL):
        for copy in range(POL):
            table[q, :, q, copy, :] = np.eye(SG)
    table = table.reshape(LANES, POL * LANES)
    return np.concatenate([table] * 3, 0).astype(ml_dtypes.bfloat16)


def unit_powers(theta):
    half = theta * 0.5
    square = half * half
    sin_h = half * (
        1.0 + square * (-1.0 / 6 + square * (1.0 / 120 + square * (-1.0 / 5040 + square * (1.0 / 362880))))
    )
    cos_h = 1.0 + square * (
        -0.5 + square * (1.0 / 24 + square * (-1.0 / 720 + square * (1.0 / 40320 + square * (-1.0 / 3628800))))
    )
    powers = {0: (jnp.ones_like(theta), jnp.zeros_like(theta))}
    powers[1] = (1.0 - 2.0 * sin_h * sin_h, 2.0 * sin_h * cos_h)
    for n in range(2, HALF + 1):
        (ca, sa), (cb, sb) = powers[n // 2], powers[n - n // 2]
        if n % 2 == 0:
            powers[n] = (1.0 - 2.0 * sa * sa, 2.0 * sa * ca)
        else:
            powers[n] = (ca * cb - sa * sb, ca * sb + sa * cb)
    return powers


def image_kernel(ks, me, valid, scales, *refs):
    blocks, uv_ref, outs = refs[: len(ks)], refs[len(ks)], refs[len(ks) + 1 : 2 * len(ks) + 1]
    u_tab, v_tab, w_tab, scale_tab = refs[2 * len(ks) + 1 :]
    lane = lax.broadcasted_iota(jnp.int32, (CHAN_G, TSTEP), 1)
    out_lane = lax.broadcasted_iota(jnp.int32, (SG, LANES), 1)
    is_re = out_lane % (2 * SG) < SG
    first_row = lax.broadcasted_iota(jnp.int32, (HALF, LANES), 0) == 0

    def build(vis_ref, s, scale):
        part = pl.ds(s * TSTEP, TSTEP)
        live = lane + s * TSTEP < valid[0, 0]
        for c in range(COMPS):
            values = vis_ref[c, :, part].astype(f32)
            w_tab[pl.ds(c * W_STEP, CHAN_G), :] = jnp.where(live, values, 0.0)
        powers = unit_powers(uv_ref[0, 0:1, part] * scale)
        for n in range(HALF):
            u_tab[pl.ds(n, CHAN_G, U_STEP), :] = powers[n][0]
            u_tab[pl.ds(HALF + n, CHAN_G, U_STEP), :] = powers[n][1]
        u_tab[pl.ds(SG, CHAN_G, U_STEP), :] = powers[HALF][0]
        u_tab[pl.ds(SG + 1, CHAN_G, U_STEP), :] = powers[HALF][1]
        powers = unit_powers(uv_ref[0, 1:2, part] * scale)
        for m in range(SG):
            cos, sin = powers[abs(m - HALF)]
            v_tab[pl.ds(m, CHAN_G, V_STEP), :] = cos
            v_tab[pl.ds(SG + m, CHAN_G, V_STEP), :] = sin if m >= HALF else -sin
        sums = None
        step = 4
        for start in range(0, CHAN_G, step):
            left, right = [], []
            for h in range(start, start + step):
                right.append(v_tab[pl.ds(h * V_STEP, 2 * SG), :].astype(bf16))
                u_rows = u_tab[pl.ds(h * U_STEP, SG), :]
                column = [
                    (u_rows * w_tab[pl.ds(c * W_STEP + h, 1), :]).astype(bf16)
                    for c in range(COMPS)
                ]
                w_all = w_tab[pl.ds(h, COMPS, W_STEP), :]
                last = [w_all * u_tab[pl.ds(h * U_STEP + SG + i, 1), :] for i in range(2)]
                column.append(jnp.concatenate(last, 0).astype(bf16))
                left.append(jnp.concatenate(column, 0))
            term = lax.dot_general(
                jnp.concatenate(left, 1),
                jnp.concatenate(right, 1),
                (((1,), (1,)), ((), ())),
                preferred_element_type=f32,
            )
            sums = term if sums is None else sums + term
        return sums

    def finish(out_ref, s, sums):
        def rows(part, pair):
            at = (part * POL + 2 * pair) * SG
            return jnp.concatenate([sums[at : at + SG], sums[at + SG : at + 2 * SG]], 1)

        def extra(sine, part, pair):
            at = COMPS * SG + COMPS * sine + part * POL + 2 * pair
            return jnp.concatenate([sums[at : at + 1], sums[at + 1 : at + 2]], 1)

        for pair in range(2):
            combine(out_ref, s, pair, rows(0, pair), rows(1, pair), functools.partial(extra, pair=pair))

    def combine(out_ref, s, pair, x, y, extra):
        xc, xs, yc, ys = x[:HALF], x[HALF:], y[:HALF], y[HALF:]
        low_re = jnp.where(first_row, extra(0, 0) + extra(1, 1), xc + ys)
        low_im = jnp.where(first_row, extra(0, 1) - extra(1, 0), yc - xs)
        f_re = jnp.concatenate([xc - ys, low_re], 0)
        f_im = jnp.concatenate([yc + xs, low_im], 0)
        swapped = jnp.where(is_re, -pltpu.roll(f_im, LANES - SG, 1), pltpu.roll(f_im, SG, 1))
        out_ref[s, pair * SG : (pair + 1) * SG, :] = (f_re + swapped).astype(bf16)

    for i, k in enumerate(ks):
        group = me[0] ^ k
        for h in range(CHAN_G):
            scale_tab[h : h + 1, :] = jnp.full((1, LANES), scales[group * CHAN_G + h], f32)
        scale = scale_tab[...] * (2.0 * math.pi / SG)
        for s in range(outs[i].shape[0]):
            finish(outs[i], s, build(blocks[i], s, scale))


def images(ks, me, valid, scales, vis, uv):
    rows = vis.shape[2]
    count = rows // TSTEP
    block = (COMPS, CHAN_G, rows)
    whole = pl.BlockSpec((count, 2 * SG, LANES), lambda i, at: (0, 0, 0))
    return pl.pallas_call(
        functools.partial(image_kernel, ks),
        out_shape=[jax.ShapeDtypeStruct((count, 2 * SG, LANES), bf16)] * len(ks),
        grid_spec=pltpu.PrefetchScalarGridSpec(
            num_scalar_prefetch=1,
            grid=(1,),
            in_specs=[smem(), smem()]
            + [pl.BlockSpec(block, lambda i, at, k=k: (0, at[0] ^ k, 0)) for k in ks]
            + [pl.BlockSpec((1, 2, rows), lambda i, at: (0, 0, 0))],
            out_specs=[whole] * len(ks),
            scratch_shapes=[
                pltpu.VMEM((CHAN_G * U_STEP, LANES), f32),
                pltpu.VMEM((CHAN_G * V_STEP, LANES), f32),
                pltpu.VMEM((COMPS * W_STEP, LANES), f32),
                pltpu.VMEM((CHAN_G, LANES), f32),
            ],
        ),
        compiler_params=pltpu.CompilerParams(vmem_limit_bytes=VMEM_LIMIT),
        cost_estimate=pl.CostEstimate(
            flops=len(ks) * count * FAN * 40000, bytes_accessed=1 << 20, transcendentals=0
        ),
        name="images",
    )(me, valid, scales, *([vis] * len(ks)), uv)


def gain_kernel(stations, aterm, taper, tiles, out_ref, rows, sems):
    count = rows.shape[0] // 2

    def copy(i):
        return pltpu.make_async_copy(
            aterm.at[0, stations[0, 0, i // count, i % count]], rows.at[i], sems.at[i]
        )

    def start(i, _):
        copy(i).start()
        return 0

    def wait(i, _):
        copy(i).wait()
        return 0

    lax.fori_loop(0, 2 * count, start, 0, unroll=8)
    lax.fori_loop(0, 2 * count, wait, 0, unroll=8)
    for r in range(SG * SG // LANES):
        cols = pl.ds(r * LANES, LANES)
        one_re, one_im = rows[0:count, 0, cols], rows[0:count, 1, cols]
        two_re, two_im = rows[count:, 0, cols], rows[count:, 1, cols]
        shape = jnp.concatenate(
            [taper[POL * r + q : POL * r + q + 1, :] for q in range(POL)], 1
        ) * (1.0 / (math.sqrt(FAN) * SG))
        gain = jnp.concatenate(
            [(one_re * two_re + one_im * two_im) * shape, (one_im * two_re - one_re * two_im) * shape], 0
        )
        high = gain.astype(bf16)
        rest = gain - high.astype(f32)
        mid = rest.astype(bf16)
        low = (rest - mid.astype(f32)).astype(bf16)
        tiled = jnp.dot(
            jnp.concatenate([high, mid, low], 1), tiles[...], preferred_element_type=f32
        )
        for q in range(POL):
            row = list(IMAGE_ROWS).index(POL * r + q)
            lanes = tiled[:, q * LANES : (q + 1) * LANES]
            out_ref[0, row] = lanes[:count]
            out_ref[1, row] = lanes[count:]


def gains(stations, aterm, taper):
    count = stations.shape[3]
    return pl.pallas_call(
        gain_kernel,
        out_shape=jax.ShapeDtypeStruct((2, SG, count, LANES), f32),
        in_specs=[smem(), pl.BlockSpec(memory_space=pl.ANY), vmem(), vmem()],
        out_specs=vmem(),
        scratch_shapes=[
            pltpu.VMEM((2 * count, 2, SG * SG), f32),
            pltpu.SemaphoreType.DMA((2 * count,)),
        ],
        compiler_params=pltpu.CompilerParams(vmem_limit_bytes=VMEM_LIMIT),
        name="gains",
    )(stations, aterm, taper, lane_tiles())


def subgrid_kernel(chunks_n, me, owner, u_offset, v_start, gain, w_high, w_low, f_rows, *refs):
    chunks = refs[:chunks_n]
    out_ref, d_high, d_low, y_ref, pos, taken = refs[chunks_n:]
    block = chunks[0].shape[0]
    row = lax.broadcasted_iota(jnp.int32, (POS_ROWS, LANES), 0)

    def clear(i, _):
        taken[i] = 0
        return 0

    lax.fori_loop(0, taken.shape[0], clear, 0, unroll=8)
    out_ref[...] = jnp.zeros_like(out_ref)
    pos[...] = jnp.full(pos.shape, NO_PLACE, f32)
    for k in range(chunks_n):
        base = (me[0] ^ k) * block
        for i in range(block):
            gain_re, gain_im = gain[0, :, base + i, :], gain[1, :, base + i, :]
            for pair in range(2):
                image = chunks[k][i, pair * SG : (pair + 1) * SG, :].astype(f32)
                both = jnp.concatenate([image * gain_re, image * gain_im], 1)
                high = both.astype(bf16)
                at = pl.ds(((k * block + i) * 2 + pair) * SG, SG)
                d_high[at, :] = high
                d_low[at, :] = (both - high.astype(f32)).astype(bf16)
    step = 256
    for i in range(d_high.shape[0] // step):
        at = pl.ds(i * step, step)
        high = d_high[at, :]
        y_ref[at, :] = (
            jnp.dot(high, w_high[...], preferred_element_type=f32)
            + jnp.dot(d_low[at, :], w_high[...], preferred_element_type=f32)
            + jnp.dot(high, w_low[...], preferred_element_type=f32)
        )
    for k in range(chunks_n):
        base = (me[0] ^ k) * block
        for i in range(block):
            at = (k * block + i) * 2 * SG
            ys = [y_ref[pl.ds(at + pair * SG, SG), :] for pair in range(2)]
            rows = jnp.concatenate(
                [
                    jnp.concatenate([y[:, :LANES] for y in ys], 1),
                    jnp.concatenate([y[:, LANES:] for y in ys], 1),
                ],
                0,
            )
            high = rows.astype(bf16)
            low = (rows - high.astype(f32)).astype(bf16)
            cells = jnp.dot(
                f_rows[...], jnp.concatenate([high, low, high], 0), preferred_element_type=f32
            ).astype(bf16)
            s = base + i
            dest = owner[0, 0, 0, s]
            slot = jnp.minimum(taken[dest], CAP - 1)
            taken[dest] = slot + 1
            for pair in range(2):
                start = pl.multiple_of((slot * 2 + pair) * SG, SG)
                out_ref[dest, pl.ds(start, SG), :] = cells[:, pair * LANES : (pair + 1) * LANES]
            u, v = u_offset[0, 0, 0, s].astype(f32), v_start[0, 0, 0, s].astype(f32)
            pos[dest] = jnp.where(row == 2 * slot, u, jnp.where(row == 2 * slot + 1, v, pos[dest]))
    out_ref[:, CAP * 2 * SG :, :] = pos[...].astype(bf16)


def subgrids(chunks, me, owner, u_offset, v_start, gain, devices_n):
    count = owner.shape[3]
    return pl.pallas_call(
        functools.partial(subgrid_kernel, len(chunks)),
        out_shape=jax.ShapeDtypeStruct((devices_n, CAP * 2 * SG + POS_ROWS, LANES), bf16),
        in_specs=[smem()] * 4 + [vmem()] * (4 + len(chunks)),
        out_specs=vmem(),
        scratch_shapes=[
            pltpu.VMEM((count * 2 * SG, 2 * LANES), bf16),
            pltpu.VMEM((count * 2 * SG, 2 * LANES), bf16),
            pltpu.VMEM((count * 2 * SG, 2 * LANES), f32),
            pltpu.VMEM((devices_n, POS_ROWS, LANES), f32),
            pltpu.SMEM((devices_n,), jnp.int32),
        ],
        compiler_params=pltpu.CompilerParams(vmem_limit_bytes=VMEM_LIMIT),
        cost_estimate=pl.CostEstimate(flops=4 * 10**9, bytes_accessed=4 << 20, transcendentals=0),
        name="subgrids",
    )(me, owner, u_offset, v_start, gain, *lane_transform(), row_transform(), *chunks)


def place_kernel(arrived, out_ref, margin_ref, columns, spread, places):
    sources = arrived.shape[0]
    per_lanes = LANES // SG
    places[...] = arrived[:, CAP * 2 * SG :, :].astype(f32)
    lane = lax.broadcasted_iota(jnp.int32, (1, LANES), 1)
    u_index = lax.broadcasted_iota(jnp.int32, (TILE_W + SG, LANES), 0).astype(f32)
    step_a = (lane % SG).astype(f32)
    for j in range(sources * CAP // per_lanes):
        target = None
        for q in range(per_lanes):
            slot = j * per_lanes + q
            u = places[slot // CAP, 2 * (slot % CAP) : 2 * (slot % CAP) + 1, :]
            target = u if target is None else jnp.where(lane < q * SG, target, u)
        hot = jnp.where(u_index == target + step_a, 1.0, 0.0)
        columns[:, j * LANES : (j + 1) * LANES] = hot.astype(bf16)
    v_index = (
        lax.broadcasted_iota(jnp.int32, (SG, BAND_V), 1) - lax.broadcasted_iota(jnp.int32, (SG, BAND_V), 0)
    ).astype(f32)

    def along_v(source, _):
        for slot in range(CAP):
            cells = arrived[source, slot * 2 * SG : (slot + 1) * 2 * SG, :]
            stacked = jnp.concatenate([cells[:, SG * k : SG * (k + 1)] for k in range(POL)], 0)
            v = places[source, 2 * slot + 1 : 2 * slot + 2, :]
            hot = jnp.where(v_index == jnp.concatenate([v, v], 1), 1.0, 0.0).astype(bf16)
            wide = jnp.dot(stacked, hot, preferred_element_type=f32).astype(bf16)
            at = pl.ds(pl.multiple_of((source * CAP + slot) * SG, SG), SG)
            for k in range(POL):
                for pair in range(2):
                    comp = (k % 2) * POL + pair * 2 + k // 2
                    start = (k * 2 + pair) * SG
                    spread[at, comp * BAND_V : (comp + 1) * BAND_V] = wide[start : start + SG]
        return 0

    lax.fori_loop(0, sources, along_v, 0, unroll=4)
    for comp in range(COMPS):
        total = jnp.dot(
            columns[...], spread[:, comp * BAND_V : (comp + 1) * BAND_V], preferred_element_type=f32
        )
        out_ref[comp] = total[:TILE_W]
        margin_ref[comp] = total[TILE_W:].astype(bf16)


def placed(arrived):
    cells = arrived.shape[0] * CAP * SG
    return pl.pallas_call(
        place_kernel,
        out_shape=(
            jax.ShapeDtypeStruct((COMPS, TILE_W, BAND_V), f32),
            jax.ShapeDtypeStruct((COMPS, SG, BAND_V), bf16),
        ),
        in_specs=[vmem()],
        out_specs=(vmem(), vmem()),
        scratch_shapes=[
            pltpu.VMEM((TILE_W + SG, cells), bf16),
            pltpu.VMEM((cells, COMPS * BAND_V), bf16),
            pltpu.VMEM((arrived.shape[0], POS_ROWS, LANES), f32),
        ],
        compiler_params=pltpu.CompilerParams(vmem_limit_bytes=VMEM_LIMIT),
        name="tile",
    )(arrived)


def on_device(
    visibilities, uv_rows, chan_scale, valid_rows, aterm, taper, stations, owner, u_offset, v_start
):
    groups_n = lax.axis_size("freq")
    devices_n = groups_n * lax.axis_size("tile")
    me = lax.axis_index("freq")[None].astype(jnp.int32)
    far = list(range(groups_n - 1, 1, -1))
    near = [k for k in (1, 0) if k < groups_n]
    chunks = {}
    for ks in (far, near):
        if ks:
            parts = images(ks, me, valid_rows, chan_scale, visibilities[0], uv_rows)
            for k, part in zip(ks, parts):
                if k:
                    part = lax.ppermute(part, "freq", [(i, i ^ k) for i in range(groups_n)])
                chunks[k] = part
    stations, owner, u_offset, v_start = (
        jnp.swapaxes(index, 2, 3) for index in (stations, owner, u_offset, v_start)
    )
    gain = gains(stations, aterm, taper)
    outgoing = subgrids(
        [chunks[k] for k in range(groups_n)], me, owner, u_offset, v_start, gain, devices_n
    )
    arrived = lax.all_to_all(
        outgoing, ("freq", "tile"), split_axis=0, concat_axis=0, tiled=True
    )
    tile, margin = placed(arrived)
    incoming = lax.ppermute(
        margin, ("freq", "tile"), [(i, (i + 1) % devices_n) for i in range(devices_n)]
    )
    return tile.at[:, :SG, :].add(incoming.astype(f32))


def solution(mesh):
    in_specs = (
        P("tile", None, None, "freq"),
        P("tile", None, "freq"),
        P(),
        P("tile", "freq"),
        P("freq", None, None, None),
        P(),
        P("tile", "freq", None, None),
        P("tile", "freq", None, None),
        P("tile", "freq", None, None),
        P("tile", "freq", None, None),
    )
    out_specs = P(None, ("freq", "tile"), None)
    return jax.shard_map(
        on_device, mesh=mesh, in_specs=in_specs, out_specs=out_specs, check_vma=False
    )
```

profile of v0, /device:TPU:0, one launch (start us, length us, event | category | flops | bytes accessed | tf_op | source)
XLA Modules:
  0.0 86.3 jit_solution(12246062892986929949)
XLA Ops:
  0.7 7.9 %images.3 = (bf16[8,64,128]{2,1,0:T(8,128)(2,1)}, bf16[8,64,128]{2,1,0:T(8,128)(2,1)}) custom-call(s32[1]{0:T(128)} %bitcast.me, s32[1,1]{1,0:T(1,128)S(6)} %copy.16.valid, f32[64]{0:T(128)} %scales.3, bf16[8,64,1024]{2,1,0:T(8,128)(2,1)} %bitcast.7, bf16[8,64,1024]{2,1,0:T(8,128)(2,1)} %bitcast.8, f32[1,2,1024]{2,1,0:T(2,128)} %refs_2_.3), custom_call_target="tpu_custom_call" | custom-call | flops 1310720000 | bytes 1048576 | tf_op jit(solution)/shard_map/images/pallas_call | solution.py:192
  8.6 2.9 %collective-permute-start.1 = (bf16[8,64,128]{2,1,0:T(8,128)(2,1)}, bf16[8,64,128]{2,1,0:T(8,128)(2,1)S(1)}, u32[]{:S(2)}, u32[]{:S(2)}) collective-permute-start(bf16[8,64,128]{2,1,0:T(8,128)(2,1)} %get-tuple-element.25), channel_id=1, source_target_pairs={{0,16},{8,24},{16,0},{24,8},{1,17},{9,25},{17,1},{25,9},{2,18},{10... | collective-permute-start | bytes 393224 | tf_op jit(solution)/shard_map/ppermute | solution.py:434
  11.5 0.0 collective-permute-start.2
  11.5 7.9 %images.2 = (bf16[8,64,128]{2,1,0:T(8,128)(2,1)}, bf16[8,64,128]{2,1,0:T(8,128)(2,1)}) custom-call(s32[1]{0:T(128)} %bitcast.me, s32[1,1]{1,0:T(1,128)S(6)} %copy.16.valid, f32[64]{0:T(128)} %scales.3, bf16[8,64,1024]{2,1,0:T(8,128)(2,1)} %bitcast.9, bf16[8,64,1024]{2,1,0:T(8,128)(2,1)} %bitcast.10, f32[1,2,1024]{2,1,0:T(2,128)} %refs_2_.3), custom_call_target="tpu_custom_call" | custom-call | flops 1310720000 | bytes 1048576 | tf_op jit(solution)/shard_map/images/pallas_call | solution.py:192
  19.4 0.1 collective-permute-start
  19.6 5.0 %gains.1.gain = f32[2,32,32,128]{3,2,1,0:T(8,128)} custom-call(s32[1,1,2,32]{3,2,1,0:T(2,128)} %bitcast.6, f32[1,512,2,1024]{3,2,1,0:T(2,128)} %aterm.1, f32[32,32]{1,0:T(8,128)} %taper.1, bf16[384,512]{1,0:T(8,128)(2,1)} %constant.40.clone.tiles), custom_call_target="tpu_custom_call" | custom-call | tf_op jit(solution)/shard_map/gains/pallas_call | solution.py:261
  24.6 0.0 collective-permute-done.1.refs_2_
  24.6 0.0 copy-start
  24.6 0.0 collective-permute-done.2.refs_3_
  24.6 0.0 copy-start.1
  24.6 0.0 collective-permute-done.refs_1_
  24.6 0.0 copy-start.2
  24.6 0.6 copy-done
  25.2 0.1 copy-done.1
  25.3 0.1 copy-done.2
  25.3 4.9 %subgrids.1 = bf16[32,136,128]{2,1,0:T(8,128)(2,1)} custom-call(s32[1]{0:T(128)} %bitcast.me, s32[1,1,1,32]{3,2,1,0:T(1,128)} %bitcast.11, s32[1,1,1,32]{3,2,1,0:T(1,128)} %bitcast.12, s32[1,1,1,32]{3,2,1,0:T(1,128)} %bitcast.13, f32[2,32,32,128]{3,2,1,0:T(8,128)} %gains.1.gain, bf16[256,256]{1,0:T(8,128)(2,1)} %constant.41.clone.w_high, ...), custom_call_target="tpu_custom_call" | custom-call | flops 4000000000 | bytes 4194304 | tf_op jit(solution)/shard_map/subgrids/pallas_call | solution.py:339
  30.2 35.6 %all_to_all.5.arrived = bf16[32,136,128]{2,1,0:T(8,128)(2,1)} all-to-all(bf16[32,136,128]{2,1,0:T(8,128)(2,1)} %subgrids.1), channel_id=1, replica_groups=mesh['freq'=4,'tile'=8] {'freq','tile'}, dimensions={0} | all-to-all | bytes 2228224 | tf_op jit(solution)/shard_map/all_to_all | solution.py:443
  65.8 9.4 %tile.1 = (f32[8,256,256]{2,1,0:T(8,128)}, bf16[8,32,256]{2,1,0:T(8,128)(2,1)}) custom-call(bf16[32,136,128]{2,1,0:T(8,128)(2,1)} %all_to_all.5.arrived), custom_call_target="tpu_custom_call" | custom-call | tf_op jit(solution)/shard_map/tile/pallas_call | solution.py:402
  75.3 0.8 collective-permute-start.3
  76.1 8.5 %collective-permute-done.3 = bf16[8,32,256]{2,1,0:T(8,128)(2,1)S(1)} collective-permute-done((bf16[8,32,256]{2,1,0:T(8,128)(2,1)}, bf16[8,32,256]{2,1,0:T(8,128)(2,1)S(1)}, u32[]{:S(2)}, u32[]{:S(2)}) %collective-permute-start.3) | collective-permute-done | bytes 131104 | tf_op jit(solution)/shard_map/ppermute | solution.py:447
  84.6 1.7 %add_dynamic-update-slice_fusion = f32[8,256,256]{2,1,0:T(8,128)} fusion(f32[8,256,256]{2,1,0:T(8,128)} %get-tuple-element.27, bf16[8,32,256]{2,1,0:T(8,128)(2,1)S(1)} %collective-permute-done.3), kind=kLoop, calls=%fused_computation | loop fusion | flops 131072 | bytes 655360 | tf_op jit(solution)/shard_map/scatter-add | solution.py:450
Async XLA Ops:
  8.6 16.0 %collective-permute-start.1 = (bf16[8,64,128]{2,1,0:T(8,128)(2,1)}, bf16[8,64,128]{2,1,0:T(8,128)(2,1)S(1)}, u32[]{:S(2)}, u32[]{:S(2)}) collective-permute-start(bf16[8,64,128]{2,1,0:T(8,128)(2,1)} %get-tuple-element.25), channel_id=1, source_target_pairs={{0,16},{8,24},{16,0},{24,8},{1,17},{9,25},{17,1},{25,9},{2,18},{10... | collective-permute-start | bytes 393224 | tf_op jit(solution)/shard_map/ppermute | solution.py:434
  11.5 13.1 %collective-permute-start.2 = (bf16[8,64,128]{2,1,0:T(8,128)(2,1)}, bf16[8,64,128]{2,1,0:T(8,128)(2,1)S(1)}, u32[]{:S(2)}, u32[]{:S(2)}) collective-permute-start(bf16[8,64,128]{2,1,0:T(8,128)(2,1)} %get-tuple-element.26), channel_id=1, source_target_pairs={{0,24},{8,16},{16,8},{24,0},{1,25},{9,17},{17,9},{25,1},{2,26},{10... | collective-permute-start | bytes 393224 | tf_op jit(solution)/shard_map/ppermute | solution.py:434
  19.4 5.2 %collective-permute-start = (bf16[8,64,128]{2,1,0:T(8,128)(2,1)}, bf16[8,64,128]{2,1,0:T(8,128)(2,1)S(1)}, u32[]{:S(2)}, u32[]{:S(2)}) collective-permute-start(bf16[8,64,128]{2,1,0:T(8,128)(2,1)} %get-tuple-element.24), channel_id=1, source_target_pairs={{0,8},{8,0},{16,24},{24,16},{1,9},{9,1},{17,25},{25,17},{2,10},{10... | collective-permute-start | bytes 393224 | tf_op jit(solution)/shard_map/ppermute | solution.py:434
  24.6 0.7 copy-start
  24.6 0.7 copy-start.1
  24.6 0.7 copy-start.2
  75.3 9.3 %collective-permute-start.3 = (bf16[8,32,256]{2,1,0:T(8,128)(2,1)}, bf16[8,32,256]{2,1,0:T(8,128)(2,1)S(1)}, u32[]{:S(2)}, u32[]{:S(2)}) collective-permute-start(bf16[8,32,256]{2,1,0:T(8,128)(2,1)} %get-tuple-element.28), channel_id=1, source_target_pairs={{0,1},{1,2},{2,3},{3,4},{4,5},{5,6},{6,7},{7,8},{8,9},{9,10},{10,1... | collective-permute-start | bytes 393224 | tf_op jit(solution)/shard_map/ppermute | solution.py:447
where the time goes:
time: 86.7 us; the launch traced here: 86.3 us
  blocking collectives  35.6 us (41%)
  Pallas kernels  35.1 us (40%)
  waiting for transfers between devices  8.49 us (10%)
  starting transfers between devices  3.92 us (5%)
  other arithmetic  1.68 us (2%)
    all_to_all x1, blocking collectives, on_device(): lax.all_to_all(outgoing, ('freq', 'tile'), split_axis=0, concat_axis=0, t...  35.6 us
    pallas_call x2, Pallas kernels, images(): pl.pallas_call(functools.partial(image_kernel, ks), out_shape=[jax.ShapeD...  15.8 us
    pallas_call x1, Pallas kernels, placed(): pl.pallas_call(place_kernel, out_shape=(jax.ShapeDtypeStruct((COMPS, TILE...  9.43 us
    ppermute x1, waiting for transfers between devices, on_device(): lax.ppermute(margin, ('freq', 'tile'), [(i, (i + 1) % devices_n) for i in...  8.48 us
    pallas_call x1, Pallas kernels, gains(): pl.pallas_call(gain_kernel, out_shape=jax.ShapeDtypeStruct((2, SG, count,...  4.98 us
    pallas_call x1, Pallas kernels, subgrids(): pl.pallas_call(functools.partial(subgrid_kernel, len(chunks)), out_shape=...  4.88 us
    ppermute x3, starting transfers between devices, on_device(): part = lax.ppermute(part, 'freq', [(i, i ^ k) for i in range(groups_n)])  3.1 us
  transfers between devices with their start and end apart: 4, of which 1 were waited for; matrix products, arithmetic and copies ran while one was open for 0% of the time, Pallas kernels for 15%

commit v1 on v0

--- a/solution.py
+++ b/solution.py
@@ -105,9 +105,56 @@
     return powers
 
 
-def image_kernel(ks, me, valid, scales, *refs):
-    blocks, uv_ref, outs = refs[: len(ks)], refs[len(ks)], refs[len(ks) + 1 : 2 * len(ks) + 1]
-    u_tab, v_tab, w_tab, scale_tab = refs[2 * len(ks) + 1 :]
+def gain_copies(stations, aterm, rows, sems):
+    count = rows.shape[0] // 2
+    return [
+        pltpu.make_async_copy(
+            aterm.at[0, stations[0, 0, i // count, i % count]], rows.at[i], sems.at[i]
+        )
+        for i in range(2 * count)
+    ]
+
+
+def make_gains(taper, tiles, out_ref, rows):
+    count = rows.shape[0] // 2
+    for r in range(SG * SG // LANES):
+        cols = pl.ds(r * LANES, LANES)
+        one_re, one_im = rows[0:count, 0, cols], rows[0:count, 1, cols]
+        two_re, two_im = rows[count:, 0, cols], rows[count:, 1, cols]
+        shape = jnp.concatenate(
+            [taper[POL * r + q : POL * r + q + 1, :] for q in range(POL)], 1
+        ) * (1.0 / (math.sqrt(FAN) * SG))
+        gain = jnp.concatenate(
+            [(one_re * two_re + one_im * two_im) * shape, (one_im * two_re - one_re * two_im) * shape], 0
+        )
+        high = gain.astype(bf16)
+        rest = gain - high.astype(f32)
+        mid = rest.astype(bf16)
+        low = (rest - mid.astype(f32)).astype(bf16)
+        tiled = jnp.dot(
+            jnp.concatenate([high, mid, low], 1), tiles[...], preferred_element_type=f32
+        )
+        for q in range(POL):
+            row = list(IMAGE_ROWS).index(POL * r + q)
+            lanes = tiled[:, q * LANES : (q + 1) * LANES]
+            out_ref[0, row] = lanes[:count]
+            out_ref[1, row] = lanes[count:]
+
+
+def image_kernel(ks, with_gains, me, valid, scales, *refs):
+    refs = list(refs)
+    take = lambda count: [refs.pop(0) for _ in range(count)]
+    stations = take(1)[0] if with_gains else None
+    blocks, (uv_ref,) = take(len(ks)), take(1)
+    aterm, taper, tiles = take(3) if with_gains else (None, None, None)
+    outs = take(len(ks))
+    gain_ref = take(1)[0] if with_gains else None
+    u_tab, v_tab, w_tab, scale_tab = take(4)
+    copies = []
+    if with_gains:
+        copies = gain_copies(stations, aterm, *refs)
+    for copy in copies:
+        copy.start()
     lane = lax.broadcasted_iota(jnp.int32, (CHAN_G, TSTEP), 1)
     out_lane = lax.broadcasted_iota(jnp.int32, (SG, LANES), 1)
     is_re = out_lane % (2 * SG) < SG
@@ -182,94 +229,57 @@
         scale = scale_tab[...] * (2.0 * math.pi / SG)
         for s in range(outs[i].shape[0]):
             finish(outs[i], s, build(blocks[i], s, scale))
-
-
-def images(ks, me, valid, scales, vis, uv):
+            if with_gains and i == len(ks) - 1 and s == outs[i].shape[0] - 3:
+                for copy in copies:
+                    copy.wait()
+                make_gains(taper, tiles, gain_ref, refs[0])
+
+
+def images(ks, me, valid, scales, vis, uv, gain_args=()):
     rows = vis.shape[2]
     count = rows // TSTEP
     block = (COMPS, CHAN_G, rows)
     whole = pl.BlockSpec((count, 2 * SG, LANES), lambda i, at: (0, 0, 0))
+    out_shape = [jax.ShapeDtypeStruct((count, 2 * SG, LANES), bf16)] * len(ks)
+    out_specs = [whole] * len(ks)
+    in_specs = [pl.BlockSpec(block, lambda i, at, k=k: (0, at[0] ^ k, 0)) for k in ks]
+    in_specs += [pl.BlockSpec((1, 2, rows), lambda i, at: (0, 0, 0))]
+    scratch = [
+        pltpu.VMEM((CHAN_G * U_STEP, LANES), f32),
+        pltpu.VMEM((CHAN_G * V_STEP, LANES), f32),
+        pltpu.VMEM((COMPS * W_STEP, LANES), f32),
+        pltpu.VMEM((CHAN_G, LANES), f32),
+    ]
+    operands = [vis] * len(ks) + [uv]
+    if gain_args:
+        stations, aterm, taper = gain_args
+        subs = stations.shape[3]
+        tiles = lane_tiles()
+        operands = [stations] + operands + [aterm, taper, tiles]
+        in_specs = [smem()] + in_specs + [
+            pl.BlockSpec(memory_space=pl.ANY),
+            pl.BlockSpec(taper.shape, lambda i, at: (0, 0)),
+            pl.BlockSpec(tiles.shape, lambda i, at: (0, 0)),
+        ]
+        out_shape += [jax.ShapeDtypeStruct((2, SG, subs, LANES), f32)]
+        out_specs += [pl.BlockSpec((2, SG, subs, LANES), lambda i, at: (0, 0, 0, 0))]
+        scratch += [pltpu.VMEM((2 * subs, 2, SG * SG), f32), pltpu.SemaphoreType.DMA((2 * subs,))]
     return pl.pallas_call(
-        functools.partial(image_kernel, ks),
-        out_shape=[jax.ShapeDtypeStruct((count, 2 * SG, LANES), bf16)] * len(ks),
+        functools.partial(image_kernel, ks, bool(gain_args)),
+        out_shape=out_shape,
         grid_spec=pltpu.PrefetchScalarGridSpec(
             num_scalar_prefetch=1,
             grid=(1,),
-            in_specs=[smem(), smem()]
-            + [pl.BlockSpec(block, lambda i, at, k=k: (0, at[0] ^ k, 0)) for k in ks]
-            + [pl.BlockSpec((1, 2, rows), lambda i, at: (0, 0, 0))],
-            out_specs=[whole] * len(ks),
-            scratch_shapes=[
-                pltpu.VMEM((CHAN_G * U_STEP, LANES), f32),
-                pltpu.VMEM((CHAN_G * V_STEP, LANES), f32),
-                pltpu.VMEM((COMPS * W_STEP, LANES), f32),
-                pltpu.VMEM((CHAN_G, LANES), f32),
-            ],
+            in_specs=[smem(), smem()] + in_specs,
+            out_specs=out_specs,
+            scratch_shapes=scratch,
         ),
         compiler_params=pltpu.CompilerParams(vmem_limit_bytes=VMEM_LIMIT),
         cost_estimate=pl.CostEstimate(
             flops=len(ks) * count * FAN * 40000, bytes_accessed=1 << 20, transcendentals=0
         ),
         name="images",
-    )(me, valid, scales, *([vis] * len(ks)), uv)
-
-
-def gain_kernel(stations, aterm, taper, tiles, out_ref, rows, sems):
-    count = rows.shape[0] // 2
-
-    def copy(i):
-        return pltpu.make_async_copy(
-            aterm.at[0, stations[0, 0, i // count, i % count]], rows.at[i], sems.at[i]
-        )
-
-    def start(i, _):
-        copy(i).start()
-        return 0
-
-    def wait(i, _):
-        copy(i).wait()
-        return 0
-
-    lax.fori_loop(0, 2 * count, start, 0, unroll=8)
-    lax.fori_loop(0, 2 * count, wait, 0, unroll=8)
-    for r in range(SG * SG // LANES):
-        cols = pl.ds(r * LANES, LANES)
-        one_re, one_im = rows[0:count, 0, cols], rows[0:count, 1, cols]
-        two_re, two_im = rows[count:, 0, cols], rows[count:, 1, cols]
-        shape = jnp.concatenate(
-            [taper[POL * r + q : POL * r + q + 1, :] for q in range(POL)], 1
-        ) * (1.0 / (math.sqrt(FAN) * SG))
-        gain = jnp.concatenate(
-            [(one_re * two_re + one_im * two_im) * shape, (one_im * two_re - one_re * two_im) * shape], 0
-        )
-        high = gain.astype(bf16)
-        rest = gain - high.astype(f32)
-        mid = rest.astype(bf16)
-        low = (rest - mid.astype(f32)).astype(bf16)
-        tiled = jnp.dot(
-            jnp.concatenate([high, mid, low], 1), tiles[...], preferred_element_type=f32
-        )
-        for q in range(POL):
-            row = list(IMAGE_ROWS).index(POL * r + q)
-            lanes = tiled[:, q * LANES : (q + 1) * LANES]
-            out_ref[0, row] = lanes[:count]
-            out_ref[1, row] = lanes[count:]
-
-
-def gains(stations, aterm, taper):
-    count = stations.shape[3]
-    return pl.pallas_call(
-        gain_kernel,
-        out_shape=jax.ShapeDtypeStruct((2, SG, count, LANES), f32),
-        in_specs=[smem(), pl.BlockSpec(memory_space=pl.ANY), vmem(), vmem()],
-        out_specs=vmem(),
-        scratch_shapes=[
-            pltpu.VMEM((2 * count, 2, SG * SG), f32),
-            pltpu.SemaphoreType.DMA((2 * count,)),
-        ],
-        compiler_params=pltpu.CompilerParams(vmem_limit_bytes=VMEM_LIMIT),
-        name="gains",
-    )(stations, aterm, taper, lane_tiles())
+    )(me, valid, scales, *operands)
 
 
 def subgrid_kernel(chunks_n, me, owner, u_offset, v_start, gain, w_high, w_low, f_rows, *refs):
@@ -354,12 +364,86 @@
     )(me, owner, u_offset, v_start, gain, *lane_transform(), row_transform(), *chunks)
 
 
-def place_kernel(arrived, out_ref, margin_ref, columns, spread, places):
+def along_v(arrived, places, source, slot, v_index):
+    cells = arrived[source, pl.ds(slot * 2 * SG, 2 * SG), :]
+    stacked = jnp.concatenate([cells[:, SG * k : SG * (k + 1)] for k in range(POL)], 0)
+    v = places[source, pl.ds(2 * slot + 1, 1), :]
+    hot = jnp.where(v_index == jnp.concatenate([v, v], 1), 1.0, 0.0).astype(bf16)
+    return jnp.dot(stacked, hot, preferred_element_type=f32)
+
+
+def v_steps():
+    rows = lax.broadcasted_iota(jnp.int32, (SG, BAND_V), 0)
+    return (lax.broadcasted_iota(jnp.int32, (SG, BAND_V), 1) - rows).astype(f32)
+
+
+def parts():
+    return [
+        ((k % 2) * POL + pair * 2 + k // 2, (k * 2 + pair) * SG) for k in range(POL) for pair in range(2)
+    ]
+
+
+def margin_kernel(arrived, out_ref, acc, places, chosen, starts):
+    sources = arrived.shape[0]
+    batch = 4
+    first = TILE_W - SG
+    acc[...] = jnp.zeros_like(acc)
+    places[...] = arrived[:, CAP * 2 * SG :, :].astype(f32)
+    found = jnp.int32(0)
+    for source in range(sources):
+        for slot in range(CAP):
+            u = places[source, 2 * slot, 0].astype(jnp.int32)
+            chosen[found] = source * CAP + slot
+            starts[found] = u - first
+            found = found + ((u > first) & (u < TILE_W)).astype(jnp.int32)
+    for i in range(batch):
+        chosen[found + i] = 0
+        starts[found + i] = 2 * SG
+    v_index = v_steps()
+
+    def add(i, _):
+        wide = []
+        for j in range(batch):
+            at = chosen[i * batch + j]
+            wide.append(along_v(arrived, places, at // CAP, at % CAP, v_index))
+        for j in range(batch):
+            rows = pl.ds(starts[i * batch + j], SG)
+            for comp, start in parts():
+                for side in range(BAND_V // LANES):
+                    acc[comp, side, rows, :] += wide[j][
+                        start : start + SG, side * LANES : (side + 1) * LANES
+                    ]
+        return 0
+
+    lax.fori_loop(0, (found + batch - 1) // batch, add, 0)
+    for side in range(BAND_V // LANES):
+        out_ref[:, :, side * LANES : (side + 1) * LANES] = acc[:, side, SG : 2 * SG, :].astype(bf16)
+
+
+def margin_of(arrived):
+    slots = arrived.shape[0] * CAP
+    return pl.pallas_call(
+        margin_kernel,
+        out_shape=jax.ShapeDtypeStruct((COMPS, SG, BAND_V), bf16),
+        in_specs=[vmem()],
+        out_specs=vmem(),
+        scratch_shapes=[
+            pltpu.VMEM((COMPS, BAND_V // LANES, 3 * SG, LANES), f32),
+            pltpu.VMEM((arrived.shape[0], POS_ROWS, LANES), f32),
+            pltpu.SMEM((slots + 4,), jnp.int32),
+            pltpu.SMEM((slots + 4,), jnp.int32),
+        ],
+        compiler_params=pltpu.CompilerParams(vmem_limit_bytes=VMEM_LIMIT),
+        name="margin",
+    )(arrived)
+
+
+def tile_kernel(arrived, out_ref, columns, spread, places, result, sems):
     sources = arrived.shape[0]
     per_lanes = LANES // SG
     places[...] = arrived[:, CAP * 2 * SG :, :].astype(f32)
     lane = lax.broadcasted_iota(jnp.int32, (1, LANES), 1)
-    u_index = lax.broadcasted_iota(jnp.int32, (TILE_W + SG, LANES), 0).astype(f32)
+    u_index = lax.broadcasted_iota(jnp.int32, (TILE_W, LANES), 0).astype(f32)
     step_a = (lane % SG).astype(f32)
     for j in range(sources * CAP // per_lanes):
         target = None
@@ -369,50 +453,47 @@
             target = u if target is None else jnp.where(lane < q * SG, target, u)
         hot = jnp.where(u_index == target + step_a, 1.0, 0.0)
         columns[:, j * LANES : (j + 1) * LANES] = hot.astype(bf16)
-    v_index = (
-        lax.broadcasted_iota(jnp.int32, (SG, BAND_V), 1) - lax.broadcasted_iota(jnp.int32, (SG, BAND_V), 0)
-    ).astype(f32)
-
-    def along_v(source, _):
-        for slot in range(CAP):
-            cells = arrived[source, slot * 2 * SG : (slot + 1) * 2 * SG, :]
-            stacked = jnp.concatenate([cells[:, SG * k : SG * (k + 1)] for k in range(POL)], 0)
-            v = places[source, 2 * slot + 1 : 2 * slot + 2, :]
-            hot = jnp.where(v_index == jnp.concatenate([v, v], 1), 1.0, 0.0).astype(bf16)
-            wide = jnp.dot(stacked, hot, preferred_element_type=f32).astype(bf16)
-            at = pl.ds(pl.multiple_of((source * CAP + slot) * SG, SG), SG)
-            for k in range(POL):
-                for pair in range(2):
-                    comp = (k % 2) * POL + pair * 2 + k // 2
-                    start = (k * 2 + pair) * SG
+    v_index = v_steps()
+    unrolled = min(32, sources)
+
+    def spread_some(i, _):
+        for j in range(unrolled):
+            source = i * unrolled + j
+            for slot in range(CAP):
+                wide = along_v(arrived, places, source, slot, v_index).astype(bf16)
+                at = pl.ds(pl.multiple_of((source * CAP + slot) * SG, SG), SG)
+                for comp, start in parts():
                     spread[at, comp * BAND_V : (comp + 1) * BAND_V] = wide[start : start + SG]
         return 0
 
-    lax.fori_loop(0, sources, along_v, 0, unroll=4)
+    lax.fori_loop(0, sources // unrolled, spread_some, 0)
+    copies = []
     for comp in range(COMPS):
-        total = jnp.dot(
+        result[comp] = jnp.dot(
             columns[...], spread[:, comp * BAND_V : (comp + 1) * BAND_V], preferred_element_type=f32
         )
-        out_ref[comp] = total[:TILE_W]
-        margin_ref[comp] = total[TILE_W:].astype(bf16)
-
-
-def placed(arrived):
+        copies.append(pltpu.make_async_copy(result.at[comp], out_ref.at[comp], sems.at[comp]))
+        copies[-1].start()
+    for copy in copies:
+        copy.wait()
+
+
+def tile_of(arrived):
     cells = arrived.shape[0] * CAP * SG
     return pl.pallas_call(
-        place_kernel,
-        out_shape=(
-            jax.ShapeDtypeStruct((COMPS, TILE_W, BAND_V), f32),
-            jax.ShapeDtypeStruct((COMPS, SG, BAND_V), bf16),
-        ),
+        tile_kernel,
+        out_shape=jax.ShapeDtypeStruct((COMPS, TILE_W, BAND_V), f32),
         in_specs=[vmem()],
-        out_specs=(vmem(), vmem()),
+        out_specs=pl.BlockSpec(memory_space=pl.ANY),
         scratch_shapes=[
-            pltpu.VMEM((TILE_W + SG, cells), bf16),
+            pltpu.VMEM((TILE_W, cells), bf16),
             pltpu.VMEM((cells, COMPS * BAND_V), bf16),
             pltpu.VMEM((arrived.shape[0], POS_ROWS, LANES), f32),
+            pltpu.VMEM((COMPS, TILE_W, BAND_V), f32),
+            pltpu.SemaphoreType.DMA((COMPS,)),
         ],
         compiler_params=pltpu.CompilerParams(vmem_limit_bytes=VMEM_LIMIT),
+        cost_estimate=pl.CostEstimate(flops=4 * 10**9, bytes_accessed=4 << 20, transcendentals=0),
         name="tile",
     )(arrived)
 
@@ -425,29 +506,32 @@
     me = lax.axis_index("freq")[None].astype(jnp.int32)
     far = list(range(groups_n - 1, 1, -1))
     near = [k for k in (1, 0) if k < groups_n]
-    chunks = {}
-    for ks in (far, near):
-        if ks:
-            parts = images(ks, me, valid_rows, chan_scale, visibilities[0], uv_rows)
-            for k, part in zip(ks, parts):
-                if k:
-                    part = lax.ppermute(part, "freq", [(i, i ^ k) for i in range(groups_n)])
-                chunks[k] = part
     stations, owner, u_offset, v_start = (
         jnp.swapaxes(index, 2, 3) for index in (stations, owner, u_offset, v_start)
     )
-    gain = gains(stations, aterm, taper)
+    chunks = {}
+
+    def make(ks, gain_args=()):
+        made = images(ks, me, valid_rows, chan_scale, visibilities[0], uv_rows, gain_args)
+        for k, part in zip(ks, made):
+            if k:
+                part = lax.ppermute(part, "freq", [(i, i ^ k) for i in range(groups_n)])
+            chunks[k] = part
+        return made[-1]
+
+    if far:
+        make(far)
+    gain = make(near, (stations, aterm, taper))
     outgoing = subgrids(
         [chunks[k] for k in range(groups_n)], me, owner, u_offset, v_start, gain, devices_n
     )
     arrived = lax.all_to_all(
         outgoing, ("freq", "tile"), split_axis=0, concat_axis=0, tiled=True
     )
-    tile, margin = placed(arrived)
     incoming = lax.ppermute(
-        margin, ("freq", "tile"), [(i, (i + 1) % devices_n) for i in range(devices_n)]
-    )
-    return tile.at[:, :SG, :].add(incoming.astype(f32))
+        margin_of(arrived), ("freq", "tile"), [(i, (i + 1) % devices_n) for i in range(devices_n)]
+    )
+    return tile_of(arrived).at[:, :SG, :].add(incoming.astype(f32))
 
 
 def solution(mesh):

time: 86.7 us -> 78.5 us (0.905)
  waiting for transfers between devices: 8.49 us -> 2.78 us
  Pallas kernels: 35.1 us -> 32.5 us
    ppermute x4, waiting for transfers between devices: 8.49 us -> 2.78 us  [the longest x3 1.4 us: make(): part = lax.ppermute(part, 'freq', [(i, i ^ k) for i in range(groups_n)])]
    pallas_call x4, Pallas kernels: 30.2 us -> 27.6 us  [the longest x2 18.3 us: images(): pl.pallas_call(functools.partial(image_kernel, ks, bool(gain_args)), out_...]
  transfers between devices with their start and end apart: 4 -> 4, of which waited for: 1 -> 2; matrix products, arithmetic and copies ran while one was open for 0% -> 0% of each run, Pallas kernels for 15% -> 22%
where the time goes in v1:
time: 78.5 us; the launch traced here: 78 us
  blocking collectives  35.4 us (45%)
  Pallas kernels  32.5 us (41%)
  starting transfers between devices  4.33 us (6%)
  waiting for transfers between devices  2.78 us (4%)
  other arithmetic  1.68 us (2%)
    all_to_all x1, blocking collectives, on_device(): lax.all_to_all(outgoing, ('freq', 'tile'), split_axis=0, concat_axis=0, t...  35.4 us
    pallas_call x2, Pallas kernels, images(): pl.pallas_call(functools.partial(image_kernel, ks, bool(gain_args)), out_...  18.3 us
    pallas_call x1, Pallas kernels, tile_of(): pl.pallas_call(tile_kernel, out_shape=jax.ShapeDtypeStruct((COMPS, TILE_W...  6.67 us
    pallas_call x1, Pallas kernels, subgrids(): pl.pallas_call(functools.partial(subgrid_kernel, len(chunks)), out_shape=...  4.89 us
    ppermute x3, starting transfers between devices, make(): part = lax.ppermute(part, 'freq', [(i, i ^ k) for i in range(groups_n)])  3.16 us
    pallas_call x1, Pallas kernels, margin_of(): pl.pallas_call(margin_kernel, out_shape=jax.ShapeDtypeStruct((COMPS, SG,...  2.67 us
    scatter-add x1, other arithmetic, on_device(): return tile_of(arrived).at[:, :SG, :].add(incoming.astype(f32))  1.68 us
  transfers between devices with their start and end apart: 4, of which 2 were waited for; matrix products, arithmetic and copies ran while one was open for 0% of the time, Pallas kernels for 22%

profile of v1, /device:TPU:0, one launch (start us, length us, event | category | flops | bytes accessed | tf_op | source)
XLA Modules:
  0.0 78.0 jit_solution(9470295649431815924)
XLA Ops:
  0.7 7.9 %images.3 = (bf16[8,64,128]{2,1,0:T(8,128)(2,1)}, bf16[8,64,128]{2,1,0:T(8,128)(2,1)}) custom-call(s32[1]{0:T(128)} %bitcast.me, s32[1,1]{1,0:T(1,128)S(6)} %copy.16.valid, f32[64]{0:T(128)} %scales.3, bf16[8,64,1024]{2,1,0:T(8,128)(2,1)} %bitcast.6, bf16[8,64,1024]{2,1,0:T(8,128)(2,1)} %bitcast.7, f32[1,2,1024]{2,1,0:T(2,128)} %refs_2_.1), custom_call_target="tpu_custom_call" | custom-call | flops 1310720000 | bytes 1048576 | tf_op jit(solution)/shard_map/images/pallas_call | solution.py:267
  8.6 2.9 %collective-permute-start.1 = (bf16[8,64,128]{2,1,0:T(8,128)(2,1)}, bf16[8,64,128]{2,1,0:T(8,128)(2,1)S(1)}, u32[]{:S(2)}, u32[]{:S(2)}) collective-permute-start(bf16[8,64,128]{2,1,0:T(8,128)(2,1)} %get-tuple-element.25), channel_id=1, source_target_pairs={{0,16},{8,24},{16,0},{24,8},{1,17},{9,25},{17,1},{25,9},{2,18},{10... | collective-permute-start | bytes 393224 | tf_op jit(solution)/shard_map/ppermute | solution.py:518
  11.5 0.0 collective-permute-start.2
  11.5 10.3 %images.2 = (bf16[8,64,128]{2,1,0:T(8,128)(2,1)}, bf16[8,64,128]{2,1,0:T(8,128)(2,1)}, f32[2,32,32,128]{3,2,1,0:T(8,128)}) custom-call(s32[1]{0:T(128)} %bitcast.me, s32[1,1]{1,0:T(1,128)S(6)} %copy.16.valid, f32[64]{0:T(128)} %scales.3, s32[1,1,2,32]{3,2,1,0:T(2,128)} %bitcast.10, bf16[8,64,1024]{2,1,0:T(8,128)(2,1)} %bitcast.8, ...), custom_call_target="tpu_custom_call" | custom-call | flops 1310720000 | bytes 1048576 | tf_op jit(solution)/shard_map/images/pallas_call | solution.py:267
  21.9 0.2 collective-permute-start
  22.1 0.0 collective-permute-done.1.refs_2_
  22.1 0.0 copy-start
  22.1 0.0 collective-permute-done.2.refs_3_
  22.1 0.0 copy-start.1
  22.1 1.4 %collective-permute-done.refs_1_ = bf16[8,64,128]{2,1,0:T(8,128)(2,1)S(1)} collective-permute-done((bf16[8,64,128]{2,1,0:T(8,128)(2,1)}, bf16[8,64,128]{2,1,0:T(8,128)(2,1)S(1)}, u32[]{:S(2)}, u32[]{:S(2)}) %collective-permute-start) | collective-permute-done | bytes 131104 | tf_op jit(solution)/shard_map/ppermute | solution.py:518
  23.5 0.0 copy-start.2
  23.5 0.0 copy-done
  23.5 0.0 copy-done.1
  23.5 0.7 copy-done.2
  24.2 4.9 %subgrids.1 = bf16[32,136,128]{2,1,0:T(8,128)(2,1)} custom-call(s32[1]{0:T(128)} %bitcast.me, s32[1,1,1,32]{3,2,1,0:T(1,128)} %bitcast.11, s32[1,1,1,32]{3,2,1,0:T(1,128)} %bitcast.12, s32[1,1,1,32]{3,2,1,0:T(1,128)} %bitcast.13, f32[2,32,32,128]{3,2,1,0:T(8,128)} %get-tuple-element.22.gain, bf16[256,256]{1,0:T(8,128)(2,1)} %constant.41.clone.w_high, ...), custom_call_target="tpu_custom_call" | custom-call | flops 4000000000 | bytes 4194304 | tf_op jit(solution)/shard_map/subgrids/pallas_call | solution.py:349
  29.0 35.4 %all_to_all.5.arrived = bf16[32,136,128]{2,1,0:T(8,128)(2,1)} all-to-all(bf16[32,136,128]{2,1,0:T(8,128)(2,1)} %subgrids.1), channel_id=1, replica_groups=mesh['freq'=4,'tile'=8] {'freq','tile'}, dimensions={0} | all-to-all | bytes 2228224 | tf_op jit(solution)/shard_map/all_to_all | solution.py:528
  64.5 2.7 %margin.1 = bf16[8,32,256]{2,1,0:T(8,128)(2,1)} custom-call(bf16[32,136,128]{2,1,0:T(8,128)(2,1)} %all_to_all.5.arrived), custom_call_target="tpu_custom_call" | custom-call | tf_op jit(solution)/shard_map/margin/pallas_call | solution.py:425
  67.1 1.2 %collective-permute-start.3 = (bf16[8,32,256]{2,1,0:T(8,128)(2,1)}, bf16[8,32,256]{2,1,0:T(8,128)(2,1)S(1)}, u32[]{:S(2)}, u32[]{:S(2)}) collective-permute-start(bf16[8,32,256]{2,1,0:T(8,128)(2,1)} %margin.1), channel_id=1, source_target_pairs={{0,1},{1,2},{2,3},{3,4},{4,5},{5,6},{6,7},{7,8},{8,9},{9,10},{10,1... | collective-permute-start | bytes 393224 | tf_op jit(solution)/shard_map/ppermute | solution.py:531
  68.3 6.7 %tile.1 = f32[8,256,256]{2,1,0:T(8,128)} custom-call(bf16[32,136,128]{2,1,0:T(8,128)(2,1)} %all_to_all.5.arrived), custom_call_target="tpu_custom_call" | custom-call | flops 4000000000 | bytes 4194304 | tf_op jit(solution)/shard_map/tile/pallas_call | solution.py:483
  75.0 1.4 %collective-permute-done.3 = bf16[8,32,256]{2,1,0:T(8,128)(2,1)S(1)} collective-permute-done((bf16[8,32,256]{2,1,0:T(8,128)(2,1)}, bf16[8,32,256]{2,1,0:T(8,128)(2,1)S(1)}, u32[]{:S(2)}, u32[]{:S(2)}) %collective-permute-start.3) | collective-permute-done | bytes 131104 | tf_op jit(solution)/shard_map/ppermute | solution.py:531
  76.4 1.7 %fusion = f32[8,256,256]{2,1,0:T(8,128)} fusion(f32[8,256,256]{2,1,0:T(8,128)} %tile.1, bf16[8,32,256]{2,1,0:T(8,128)(2,1)S(1)} %collective-permute-done.3), kind=kLoop, calls=%fused_computation.1 | loop fusion | flops 131072 | bytes 655360 | tf_op jit(solution)/shard_map/scatter-add | solution.py:534
Async XLA Ops:
  8.6 13.5 %collective-permute-start.1 = (bf16[8,64,128]{2,1,0:T(8,128)(2,1)}, bf16[8,64,128]{2,1,0:T(8,128)(2,1)S(1)}, u32[]{:S(2)}, u32[]{:S(2)}) collective-permute-start(bf16[8,64,128]{2,1,0:T(8,128)(2,1)} %get-tuple-element.25), channel_id=1, source_target_pairs={{0,16},{8,24},{16,0},{24,8},{1,17},{9,25},{17,1},{25,9},{2,18},{10... | collective-permute-start | bytes 393224 | tf_op jit(solution)/shard_map/ppermute | solution.py:518
  11.5 10.6 %collective-permute-start.2 = (bf16[8,64,128]{2,1,0:T(8,128)(2,1)}, bf16[8,64,128]{2,1,0:T(8,128)(2,1)S(1)}, u32[]{:S(2)}, u32[]{:S(2)}) collective-permute-start(bf16[8,64,128]{2,1,0:T(8,128)(2,1)} %get-tuple-element.26), channel_id=1, source_target_pairs={{0,24},{8,16},{16,8},{24,0},{1,25},{9,17},{17,9},{25,1},{2,26},{10... | collective-permute-start | bytes 393224 | tf_op jit(solution)/shard_map/ppermute | solution.py:518
  21.9 1.6 %collective-permute-start = (bf16[8,64,128]{2,1,0:T(8,128)(2,1)}, bf16[8,64,128]{2,1,0:T(8,128)(2,1)S(1)}, u32[]{:S(2)}, u32[]{:S(2)}) collective-permute-start(bf16[8,64,128]{2,1,0:T(8,128)(2,1)} %get-tuple-element.24), channel_id=1, source_target_pairs={{0,8},{8,0},{16,24},{24,16},{1,9},{9,1},{17,25},{25,17},{2,10},{10... | collective-permute-start | bytes 393224 | tf_op jit(solution)/shard_map/ppermute | solution.py:518
  22.1 1.4 %copy-start = (bf16[8,64,128]{2,1,0:T(8,128)(2,1)}, bf16[8,64,128]{2,1,0:T(8,128)(2,1)S(1)}, u32[]{:S(2)}) copy-start(bf16[8,64,128]{2,1,0:T(8,128)(2,1)S(1)} %collective-permute-done.1.refs_2_) | copy-start | bytes 393220
  22.1 1.4 %copy-start.1 = (bf16[8,64,128]{2,1,0:T(8,128)(2,1)}, bf16[8,64,128]{2,1,0:T(8,128)(2,1)S(1)}, u32[]{:S(2)}) copy-start(bf16[8,64,128]{2,1,0:T(8,128)(2,1)S(1)} %collective-permute-done.2.refs_3_) | copy-start | bytes 393220
  23.5 0.7 copy-start.2
  67.1 9.2 %collective-permute-start.3 = (bf16[8,32,256]{2,1,0:T(8,128)(2,1)}, bf16[8,32,256]{2,1,0:T(8,128)(2,1)S(1)}, u32[]{:S(2)}, u32[]{:S(2)}) collective-permute-start(bf16[8,32,256]{2,1,0:T(8,128)(2,1)} %margin.1), channel_id=1, source_target_pairs={{0,1},{1,2},{2,3},{3,4},{4,5},{5,6},{6,7},{7,8},{8,9},{9,10},{10,1... | collective-permute-start | bytes 393224 | tf_op jit(solution)/shard_map/ppermute | solution.py:531

commit v2 on v1

--- a/solution.py
+++ b/solution.py
@@ -22,9 +22,12 @@
 POL = 4
 POS_ROWS = 8
 NO_PLACE = 512.0
+COARSE = (4, 12)
+FINE = 4
+SUMS = 2 * (FINE + 1) * COMPS
 CAP = 2
 U_STEP = SG + 3
-V_STEP = 2 * SG + 1
+V_STEP = 13
 W_STEP = CHAN_G + 1
 VMEM_LIMIT = 60 << 20
 f32 = jnp.float32
@@ -76,6 +79,26 @@
     return np.concatenate([high, high, low], 1)
 
 
+def combine_table():
+    table = np.zeros((4, 2, LANES, 2, 2, 2, SG))
+    for m in range(SG):
+        for a, coarse in enumerate((COARSE[0], -COARSE[0], COARSE[1], -COARSE[1])):
+            b = m - HALF - coarse
+            if not -FINE <= b < FINE:
+                continue
+            size, sign = abs(b), 1 if b > 0 else -1
+            for p in range(POL):
+                re, im = table[a, :, :, p // 2, p % 2, 0, m], table[a, :, :, p // 2, p % 2, 1, m]
+                at = 2 * FINE * COMPS if b == 0 else (size - 1) * COMPS
+                re[0, at + p], im[0, at + POL + p] = 1, 1
+                re[1, at + POL + p], im[1, at + p] = -1, 1
+                if b:
+                    at += FINE * COMPS
+                    re[0, at + POL + p], im[0, at + p] = -sign, sign
+                    re[1, at + p], im[1, at + POL + p] = -sign, -sign
+    return table.reshape(8 * LANES, 2 * LANES).astype(ml_dtypes.bfloat16)
+
+
 def lane_tiles():
     table = np.zeros((POL, SG, POL, POL, SG))
     for q in range(POL):
@@ -85,7 +108,7 @@
     return np.concatenate([table] * 3, 0).astype(ml_dtypes.bfloat16)
 
 
-def unit_powers(theta):
+def unit_powers(theta, wanted):
     half = theta * 0.5
     square = half * half
     sin_h = half * (
@@ -96,9 +119,12 @@
     )
     powers = {0: (jnp.ones_like(theta), jnp.zeros_like(theta))}
     powers[1] = (1.0 - 2.0 * sin_h * sin_h, 2.0 * sin_h * cos_h)
-    for n in range(2, HALF + 1):
-        (ca, sa), (cb, sb) = powers[n // 2], powers[n - n // 2]
-        if n % 2 == 0:
+    for n in wanted:
+        if n in powers:
+            continue
+        first = n // 2 if n != 12 else 4
+        (ca, sa), (cb, sb) = powers[first], powers[n - first]
+        if 2 * first == n:
             powers[n] = (1.0 - 2.0 * sa * sa, 2.0 * sa * ca)
         else:
             powers[n] = (ca * cb - sa * sb, ca * sb + sa * cb)
@@ -109,7 +135,9 @@
     count = rows.shape[0] // 2
     return [
         pltpu.make_async_copy(
-            aterm.at[0, stations[0, 0, i // count, i % count]], rows.at[i], sems.at[i]
+            aterm.at[0, stations[0, 0, i // count, i % count]],
+            rows.at[i, :, pl.ds(0, SG * SG)],
+            sems.at[i],
         )
         for i in range(2 * count)
     ]
@@ -117,7 +145,9 @@
 
 def make_gains(taper, tiles, out_ref, rows):
     count = rows.shape[0] // 2
-    for r in range(SG * SG // LANES):
+    blocks = SG * SG // LANES
+    parts = []
+    for r in range(blocks):
         cols = pl.ds(r * LANES, LANES)
         one_re, one_im = rows[0:count, 0, cols], rows[0:count, 1, cols]
         two_re, two_im = rows[count:, 0, cols], rows[count:, 1, cols]
@@ -131,67 +161,73 @@
         rest = gain - high.astype(f32)
         mid = rest.astype(bf16)
         low = (rest - mid.astype(f32)).astype(bf16)
-        tiled = jnp.dot(
-            jnp.concatenate([high, mid, low], 1), tiles[...], preferred_element_type=f32
-        )
+        parts.append(jnp.concatenate([high, mid, low], 1))
+    tiled = jnp.dot(jnp.concatenate(parts, 0), tiles[...], preferred_element_type=f32)
+    for r in range(blocks):
         for q in range(POL):
             row = list(IMAGE_ROWS).index(POL * r + q)
-            lanes = tiled[:, q * LANES : (q + 1) * LANES]
-            out_ref[0, row] = lanes[:count]
-            out_ref[1, row] = lanes[count:]
+            for part in range(2):
+                at = (2 * r + part) * count
+                out_ref[part, row] = tiled[at : at + count, q * LANES : (q + 1) * LANES]
 
 
 def image_kernel(ks, with_gains, me, valid, scales, *refs):
     refs = list(refs)
     take = lambda count: [refs.pop(0) for _ in range(count)]
     stations = take(1)[0] if with_gains else None
-    blocks, (uv_ref,) = take(len(ks)), take(1)
+    vis_ref, uv_ref, combine = take(3)
     aterm, taper, tiles = take(3) if with_gains else (None, None, None)
     outs = take(len(ks))
     gain_ref = take(1)[0] if with_gains else None
-    u_tab, v_tab, w_tab, scale_tab = take(4)
-    copies = []
-    if with_gains:
-        copies = gain_copies(stations, aterm, *refs)
-    for copy in copies:
-        copy.start()
+    u_tabs, v_tabs, w_tabs, scale_tab, x_high, x_low = take(6)
+    turn = pl.program_id(0)
+    copies = gain_copies(stations, aterm, *refs) if with_gains else []
+
+    @pl.when(turn == 0)
+    def _():
+        for copy in copies:
+            copy.start()
+
     lane = lax.broadcasted_iota(jnp.int32, (CHAN_G, TSTEP), 1)
-    out_lane = lax.broadcasted_iota(jnp.int32, (SG, LANES), 1)
-    is_re = out_lane % (2 * SG) < SG
     first_row = lax.broadcasted_iota(jnp.int32, (HALF, LANES), 0) == 0
 
-    def build(vis_ref, s, scale):
+    def build(s, scale):
+        u_tab, v_tab, w_tab = u_tabs.at[s % 2], v_tabs.at[s % 2], w_tabs.at[s % 2]
         part = pl.ds(s * TSTEP, TSTEP)
         live = lane + s * TSTEP < valid[0, 0]
         for c in range(COMPS):
             values = vis_ref[c, :, part].astype(f32)
             w_tab[pl.ds(c * W_STEP, CHAN_G), :] = jnp.where(live, values, 0.0)
-        powers = unit_powers(uv_ref[0, 0:1, part] * scale)
+        powers = unit_powers(uv_ref[0, 0:1, part] * scale, range(HALF + 1))
         for n in range(HALF):
             u_tab[pl.ds(n, CHAN_G, U_STEP), :] = powers[n][0]
             u_tab[pl.ds(HALF + n, CHAN_G, U_STEP), :] = powers[n][1]
         u_tab[pl.ds(SG, CHAN_G, U_STEP), :] = powers[HALF][0]
         u_tab[pl.ds(SG + 1, CHAN_G, U_STEP), :] = powers[HALF][1]
-        powers = unit_powers(uv_ref[0, 1:2, part] * scale)
-        for m in range(SG):
-            cos, sin = powers[abs(m - HALF)]
-            v_tab[pl.ds(m, CHAN_G, V_STEP), :] = cos
-            v_tab[pl.ds(SG + m, CHAN_G, V_STEP), :] = sin if m >= HALF else -sin
+        powers = unit_powers(uv_ref[0, 1:2, part] * scale, (1, 2, 3, 4, 8, 12))
+        for q, n in enumerate(COARSE):
+            v_tab[pl.ds(2 * q, CHAN_G, V_STEP), :] = powers[n][0]
+            v_tab[pl.ds(2 * q + 1, CHAN_G, V_STEP), :] = powers[n][1]
+        for n in range(1, FINE + 1):
+            v_tab[pl.ds(3 + n, CHAN_G, V_STEP), :] = powers[n][0]
+            v_tab[pl.ds(3 + FINE + n, CHAN_G, V_STEP), :] = powers[n][1]
         sums = None
         step = 4
+        pad = jnp.zeros((COMPS, TSTEP), f32)
         for start in range(0, CHAN_G, step):
             left, right = [], []
             for h in range(start, start + step):
-                right.append(v_tab[pl.ds(h * V_STEP, 2 * SG), :].astype(bf16))
                 u_rows = u_tab[pl.ds(h * U_STEP, SG), :]
                 column = [
-                    (u_rows * w_tab[pl.ds(c * W_STEP + h, 1), :]).astype(bf16)
-                    for c in range(COMPS)
+                    (u_rows * v_tab[pl.ds(h * V_STEP + a, 1), :]).astype(bf16) for a in range(4)
                 ]
+                coarse = v_tab[pl.ds(h * V_STEP, 4), :]
+                last = [coarse * u_tab[pl.ds(h * U_STEP + SG + i, 1), :] for i in range(2)]
+                column.append(jnp.concatenate(last + [pad], 0).astype(bf16))
+                left.append(jnp.concatenate(column, 0))
                 w_all = w_tab[pl.ds(h, COMPS, W_STEP), :]
-                last = [w_all * u_tab[pl.ds(h * U_STEP + SG + i, 1), :] for i in range(2)]
-                column.append(jnp.concatenate(last, 0).astype(bf16))
-                left.append(jnp.concatenate(column, 0))
+                fine = [w_all * v_tab[pl.ds(h * V_STEP + 4 + b, 1), :] for b in range(2 * FINE)]
+                right.append(jnp.concatenate(fine + [w_all, pad], 0).astype(bf16))
             term = lax.dot_general(
                 jnp.concatenate(left, 1),
                 jnp.concatenate(right, 1),
@@ -201,38 +237,56 @@
             sums = term if sums is None else sums + term
         return sums
 
-    def finish(out_ref, s, sums):
-        def rows(part, pair):
-            at = (part * POL + 2 * pair) * SG
-            return jnp.concatenate([sums[at : at + SG], sums[at + SG : at + 2 * SG]], 1)
-
-        def extra(sine, part, pair):
-            at = COMPS * SG + COMPS * sine + part * POL + 2 * pair
-            return jnp.concatenate([sums[at : at + 1], sums[at + 1 : at + 2]], 1)
-
-        for pair in range(2):
-            combine(out_ref, s, pair, rows(0, pair), rows(1, pair), functools.partial(extra, pair=pair))
-
-    def combine(out_ref, s, pair, x, y, extra):
-        xc, xs, yc, ys = x[:HALF], x[HALF:], y[:HALF], y[HALF:]
-        low_re = jnp.where(first_row, extra(0, 0) + extra(1, 1), xc + ys)
-        low_im = jnp.where(first_row, extra(0, 1) - extra(1, 0), yc - xs)
-        f_re = jnp.concatenate([xc - ys, low_re], 0)
-        f_im = jnp.concatenate([yc + xs, low_im], 0)
-        swapped = jnp.where(is_re, -pltpu.roll(f_im, LANES - SG, 1), pltpu.roll(f_im, SG, 1))
-        out_ref[s, pair * SG : (pair + 1) * SG, :] = (f_re + swapped).astype(bf16)
-
-    for i, k in enumerate(ks):
-        group = me[0] ^ k
-        for h in range(CHAN_G):
-            scale_tab[h : h + 1, :] = jnp.full((1, LANES), scales[group * CHAN_G + h], f32)
-        scale = scale_tab[...] * (2.0 * math.pi / SG)
-        for s in range(outs[i].shape[0]):
-            finish(outs[i], s, build(blocks[i], s, scale))
-            if with_gains and i == len(ks) - 1 and s == outs[i].shape[0] - 3:
-                for copy in copies:
-                    copy.wait()
-                make_gains(taper, tiles, gain_ref, refs[0])
+    def keep(s, sums):
+        top = 4 * SG
+        sums = jnp.concatenate([sums, jnp.zeros((sums.shape[0], LANES - SUMS), f32)], 1)
+        for q in range(2):
+            cos, sin = sums[2 * q * SG : (2 * q + 1) * SG], sums[(2 * q + 1) * SG : (2 * q + 2) * SG]
+            cc, sc, cs, ss = cos[:HALF], cos[HALF:], sin[:HALF], sin[HALF:]
+            ends = [sums[top + e : top + e + 1] for e in (2 * q, 4 + 2 * q, 2 * q + 1, 5 + 2 * q)]
+            ecc, esc, ecs, ess = [jnp.where(first_row, e, x) for e, x in zip(ends, (cc, sc, cs, ss))]
+            for d, (zero, one) in enumerate(
+                (
+                    ((cc - ss, ecc + ess), (sc + cs, ecs - esc)),
+                    ((cc + ss, ecc - ess), (sc - cs, -esc - ecs)),
+                )
+            ):
+                for x, values in enumerate((zero, one)):
+                    both = jnp.concatenate(values, 0)
+                    high = both.astype(bf16)
+                    at = ((2 * q + d) * 2 + x) * LANES
+                    x_high[s * SG : (s + 1) * SG, at : at + LANES] = high
+                    x_low[s * SG : (s + 1) * SG, at : at + LANES] = (both - high.astype(f32)).astype(bf16)
+
+    group = me[0] ^ (ks[0] - turn)
+    for h in range(CHAN_G):
+        scale_tab[h : h + 1, :] = jnp.full((1, LANES), scales[group * CHAN_G + h], f32)
+    scale = scale_tab[...] * (2.0 * math.pi / SG)
+    count = outs[0].shape[0]
+    for s in range(count):
+        keep(s, build(s, scale))
+    image = (
+        jnp.dot(x_high[...], combine[...], preferred_element_type=f32)
+        + jnp.dot(x_low[...], combine[...], preferred_element_type=f32)
+    ).astype(bf16)
+
+    def write(out_ref):
+        for s in range(count):
+            for pair in range(2):
+                out_ref[s, pair * SG : (pair + 1) * SG, :] = image[
+                    s * SG : (s + 1) * SG, pair * LANES : (pair + 1) * LANES
+                ]
+
+    for i, out_ref in enumerate(outs):
+        pl.when(turn == i)(functools.partial(write, out_ref))
+
+    if with_gains:
+
+        @pl.when(turn == len(ks) - 1)
+        def _():
+            for copy in copies:
+                copy.wait()
+            make_gains(taper, tiles, gain_ref, refs[0])
 
 
 def images(ks, me, valid, scales, vis, uv, gain_args=()):
@@ -242,15 +296,21 @@
     whole = pl.BlockSpec((count, 2 * SG, LANES), lambda i, at: (0, 0, 0))
     out_shape = [jax.ShapeDtypeStruct((count, 2 * SG, LANES), bf16)] * len(ks)
     out_specs = [whole] * len(ks)
-    in_specs = [pl.BlockSpec(block, lambda i, at, k=k: (0, at[0] ^ k, 0)) for k in ks]
-    in_specs += [pl.BlockSpec((1, 2, rows), lambda i, at: (0, 0, 0))]
+    in_specs = [pl.BlockSpec(block, lambda i, at: (0, at[0] ^ (ks[0] - i), 0))]
+    table = combine_table()
+    in_specs += [
+        pl.BlockSpec((1, 2, rows), lambda i, at: (0, 0, 0)),
+        pl.BlockSpec(table.shape, lambda i, at: (0, 0)),
+    ]
     scratch = [
-        pltpu.VMEM((CHAN_G * U_STEP, LANES), f32),
-        pltpu.VMEM((CHAN_G * V_STEP, LANES), f32),
-        pltpu.VMEM((COMPS * W_STEP, LANES), f32),
+        pltpu.VMEM((2, CHAN_G * U_STEP, LANES), f32),
+        pltpu.VMEM((2, CHAN_G * V_STEP, LANES), f32),
+        pltpu.VMEM((2, COMPS * W_STEP, LANES), f32),
         pltpu.VMEM((CHAN_G, LANES), f32),
+        pltpu.VMEM((count * SG, 8 * LANES), bf16),
+        pltpu.VMEM((count * SG, 8 * LANES), bf16),
     ]
-    operands = [vis] * len(ks) + [uv]
+    operands = [vis, uv, table]
     if gain_args:
         stations, aterm, taper = gain_args
         subs = stations.shape[3]
@@ -263,13 +323,13 @@
         ]
         out_shape += [jax.ShapeDtypeStruct((2, SG, subs, LANES), f32)]
         out_specs += [pl.BlockSpec((2, SG, subs, LANES), lambda i, at: (0, 0, 0, 0))]
-        scratch += [pltpu.VMEM((2 * subs, 2, SG * SG), f32), pltpu.SemaphoreType.DMA((2 * subs,))]
+        scratch += [pltpu.VMEM((2 * subs, 2, SG * SG + LANES), f32), pltpu.SemaphoreType.DMA((2 * subs,))]
     return pl.pallas_call(
         functools.partial(image_kernel, ks, bool(gain_args)),
         out_shape=out_shape,
         grid_spec=pltpu.PrefetchScalarGridSpec(
             num_scalar_prefetch=1,
-            grid=(1,),
+            grid=(len(ks),),
             in_specs=[smem(), smem()] + in_specs,
             out_specs=out_specs,
             scratch_shapes=scratch,
@@ -358,7 +418,7 @@
             pltpu.VMEM((devices_n, POS_ROWS, LANES), f32),
             pltpu.SMEM((devices_n,), jnp.int32),
         ],
-        compiler_params=pltpu.CompilerParams(vmem_limit_bytes=VMEM_LIMIT),
+        compiler_params=pltpu.CompilerParams(vmem_limit_bytes=24 << 20),
         cost_estimate=pl.CostEstimate(flops=4 * 10**9, bytes_accessed=4 << 20, transcendentals=0),
         name="subgrids",
     )(me, owner, u_offset, v_start, gain, *lane_transform(), row_transform(), *chunks)
@@ -433,7 +493,7 @@
             pltpu.SMEM((slots + 4,), jnp.int32),
             pltpu.SMEM((slots + 4,), jnp.int32),
         ],
-        compiler_params=pltpu.CompilerParams(vmem_limit_bytes=VMEM_LIMIT),
+        compiler_params=pltpu.CompilerParams(vmem_limit_bytes=16 << 20),
         name="margin",
     )(arrived)
 
@@ -492,7 +552,7 @@
             pltpu.VMEM((COMPS, TILE_W, BAND_V), f32),
             pltpu.SemaphoreType.DMA((COMPS,)),
         ],
-        compiler_params=pltpu.CompilerParams(vmem_limit_bytes=VMEM_LIMIT),
+        compiler_params=pltpu.CompilerParams(vmem_limit_bytes=(10 << 20) + 2 * cells * (COMPS * BAND_V + 2 * TILE_W)),
         cost_estimate=pl.CostEstimate(flops=4 * 10**9, bytes_accessed=4 << 20, transcendentals=0),
         name="tile",
     )(arrived)

time: 78.5 us -> 73.1 us (0.931)
  Pallas kernels: 32.5 us -> 24.8 us
  waiting for transfers between devices: 2.78 us -> 4.33 us
  local copies, waits for them, and re-layouts: 0.67 us -> 2.16 us
    pallas_call x2, Pallas kernels: 18.3 us -> 15.3 us  [images(): pl.pallas_call(functools.partial(image_kernel, ks, bool(gain_args)), out_...]
    pallas_call x1, Pallas kernels: 4.89 us -> 2.93 us  [subgrids(): pl.pallas_call(functools.partial(subgrid_kernel, len(chunks)), out_shape=...]
    ppermute x1, waiting for transfers between devices: 1.38 us -> 2.94 us  [on_device(): lax.ppermute(margin_of(arrived), ('freq', 'tile'), [(i, (i + 1) % devices...]
    pallas_call x1, Pallas kernels: 2.67 us -> 1.13 us  [margin_of(): pl.pallas_call(margin_kernel, out_shape=jax.ShapeDtypeStruct((COMPS, SG,...]
    unnamed x6 -> x16, local copies, waits for them, and re-layouts: 0.67 us -> 2.16 us
    pallas_call x1, Pallas kernels: 6.67 us -> 5.43 us  [tile_of(): pl.pallas_call(tile_kernel, out_shape=jax.ShapeDtypeStruct((COMPS, TILE_W...]
  transfers between devices with their start and end apart: 4 -> 4, of which waited for: 2 -> 2; matrix products, arithmetic and copies ran while one was open for 0% -> 0% of each run, Pallas kernels for 22% -> 20%
where the time goes in v2:
time: 73.1 us; the launch traced here: 72.7 us
  blocking collectives  35.1 us (48%)
  Pallas kernels  24.8 us (34%)
  waiting for transfers between devices  4.33 us (6%)
  starting transfers between devices  3.87 us (5%)
  local copies, waits for them, and re-layouts  2.16 us (3%)
  other arithmetic  1.68 us (2%)
  between operations  0.76 us (1%)
    all_to_all x1, blocking collectives, on_device(): lax.all_to_all(outgoing, ('freq', 'tile'), split_axis=0, concat_axis=0, t...  35.1 us
    pallas_call x2, Pallas kernels, images(): pl.pallas_call(functools.partial(image_kernel, ks, bool(gain_args)), out_...  15.3 us
    pallas_call x1, Pallas kernels, tile_of(): pl.pallas_call(tile_kernel, out_shape=jax.ShapeDtypeStruct((COMPS, TILE_W...  5.43 us
    ppermute x3, starting transfers between devices, make(): part = lax.ppermute(part, 'freq', [(i, i ^ k) for i in range(groups_n)])  3.17 us
    ppermute x1, waiting for transfers between devices, on_device(): lax.ppermute(margin_of(arrived), ('freq', 'tile'), [(i, (i + 1) % devices...  2.94 us
    pallas_call x1, Pallas kernels, subgrids(): pl.pallas_call(functools.partial(subgrid_kernel, len(chunks)), out_shape=...  2.93 us
    unnamed x16, local copies, waits for them, and re-layouts  2.16 us
    scatter-add x1, other arithmetic, on_device(): return tile_of(arrived).at[:, :SG, :].add(incoming.astype(f32))  1.68 us
  transfers between devices with their start and end apart: 4, of which 2 were waited for; matrix products, arithmetic and copies ran while one was open for 0% of the time, Pallas kernels for 20%

profile of v2, /device:TPU:0, one launch (start us, length us, event | category | flops | bytes accessed | tf_op | source)
XLA Modules:
  0.0 72.7 jit_solution(12149023677303353181)
XLA Ops:
  0.7 6.5 %images.3 = (bf16[8,64,128]{2,1,0:T(8,128)(2,1)}, bf16[8,64,128]{2,1,0:T(8,128)(2,1)}) custom-call(s32[1]{0:T(128)} %bitcast.me, s32[1,1]{1,0:T(1,128)S(6)} %copy.18.valid, f32[64]{0:T(128)} %scales.3, bf16[8,64,1024]{2,1,0:T(8,128)(2,1)} %bitcast.9, f32[1,2,1024]{2,1,0:T(2,128)} %refs_1_.1, bf16[1024,256]{1,0:T(8,128)(2,1)} %constant.42.clone.refs_3_.refs_2_), custom_call_target="tpu_custom_call" | custom-call | flops 1310720000 | bytes 1048576 | tf_op jit(solution)/shard_map/images/pallas_call | solution.py:327
  7.2 2.9 %collective-permute-start.1 = (bf16[8,64,128]{2,1,0:T(8,128)(2,1)}, bf16[8,64,128]{2,1,0:T(8,128)(2,1)S(1)}, u32[]{:S(2)}, u32[]{:S(2)}) collective-permute-start(bf16[8,64,128]{2,1,0:T(8,128)(2,1)} %get-tuple-element.25), channel_id=1, source_target_pairs={{0,16},{8,24},{16,0},{24,8},{1,17},{9,25},{17,1},{25,9},{2,18},{10... | collective-permute-start | bytes 393224 | tf_op jit(solution)/shard_map/ppermute | solution.py:578
  10.1 0.0 collective-permute-start.2
  10.1 0.0 copy-start.2
  10.1 0.0 copy-start.3
  10.1 0.0 copy-start.4
  10.1 0.0 copy-start.5
  10.1 0.0 copy-start.6
  10.2 0.0 copy-start.7
  10.2 8.8 %images.2 = (bf16[8,64,128]{2,1,0:T(8,128)(2,1)}, bf16[8,64,128]{2,1,0:T(8,128)(2,1)}, f32[2,32,32,128]{3,2,1,0:T(8,128)}) custom-call(s32[1]{0:T(128)} %bitcast.me, s32[1,1]{1,0:T(1,128)S(6)} %copy.18.valid, f32[64]{0:T(128)} %scales.3, s32[1,1,2,32]{3,2,1,0:T(2,128)} %bitcast.11, bf16[8,64,1024]{2,1,0:T(8,128)(2,1)} %bitcast.10, f32[1,2,1024]{2,1,0:T(2,128)} %refs_1_.1, ...), custom_call_target="tpu_custom_call" | custom-call | flops 1310720000 | bytes 1048576 | tf_op jit(solution)/shard_map/images/pallas_call | solution.py:327
  18.9 0.2 collective-permute-start
  19.2 0.0 collective-permute-done.1.refs_2_
  19.2 0.0 collective-permute-done.2.refs_3_
  19.2 1.4 %collective-permute-done.refs_1_ = bf16[8,64,128]{2,1,0:T(8,128)(2,1)S(1)} collective-permute-done((bf16[8,64,128]{2,1,0:T(8,128)(2,1)}, bf16[8,64,128]{2,1,0:T(8,128)(2,1)S(1)}, u32[]{:S(2)}, u32[]{:S(2)}) %collective-permute-start) | collective-permute-done | bytes 131104 | tf_op jit(solution)/shard_map/ppermute | solution.py:578
  20.6 0.0 copy-done.2
  20.6 0.0 copy-done.3
  20.6 0.0 copy-done.4
  20.6 0.0 copy-done.5
  20.6 0.0 copy-done.6
  20.6 0.0 copy-done.7
  20.6 0.0 copy-start
  20.6 1.2 %copy-done = f32[2,32,32,128]{3,2,1,0:T(8,128)S(1)} copy-done((f32[2,32,32,128]{3,2,1,0:T(8,128)S(1)}, f32[2,32,32,128]{3,2,1,0:T(8,128)}, u32[]{:S(2)}) %copy-start) | copy-done | bytes 1048600
  21.8 0.0 copy-start.1
  21.8 0.9 %copy-done.1 = bf16[8,64,128]{2,1,0:T(8,128)(2,1)S(1)} copy-done((bf16[8,64,128]{2,1,0:T(8,128)(2,1)S(1)}, bf16[8,64,128]{2,1,0:T(8,128)(2,1)}, u32[]{:S(2)}) %copy-start.1) | copy-done | bytes 131096
  22.7 2.9 %subgrids.1 = bf16[32,136,128]{2,1,0:T(8,128)(2,1)S(1)} custom-call(s32[1]{0:T(128)} %bitcast.me, s32[1,1,1,32]{3,2,1,0:T(1,128)S(1)} %bitcast.6, s32[1,1,1,32]{3,2,1,0:T(1,128)S(1)} %bitcast.7, s32[1,1,1,32]{3,2,1,0:T(1,128)S(1)} %bitcast.8, f32[2,32,32,128]{3,2,1,0:T(8,128)S(1)} %copy-done, bf16[256,256]{1,0:T(8,128)(2,1)S(1)} %copy-done.6, ...), custom_call_target="tpu_custom_call" | custom-call | flops 4000000000 | bytes 4194304 | tf_op jit(solution)/shard_map/subgrids/pallas_call | solution.py:409
  25.7 35.1 %all_to_all.5.arrived = bf16[32,136,128]{2,1,0:T(8,128)(2,1)S(1)} all-to-all(bf16[32,136,128]{2,1,0:T(8,128)(2,1)S(1)} %subgrids.1), channel_id=1, replica_groups=mesh['freq'=4,'tile'=8] {'freq','tile'}, dimensions={0} | all-to-all | bytes 2228224 | tf_op jit(solution)/shard_map/all_to_all | solution.py:588
  60.8 1.1 %margin.1 = bf16[8,32,256]{2,1,0:T(8,128)(2,1)S(1)} custom-call(bf16[32,136,128]{2,1,0:T(8,128)(2,1)S(1)} %all_to_all.5.arrived), custom_call_target="tpu_custom_call" | custom-call | tf_op jit(solution)/shard_map/margin/pallas_call | solution.py:485
  62.0 0.7 collective-permute-start.3
  62.7 5.4 %tile.1 = f32[8,256,256]{2,1,0:T(8,128)} custom-call(bf16[32,136,128]{2,1,0:T(8,128)(2,1)S(1)} %all_to_all.5.arrived), custom_call_target="tpu_custom_call" | custom-call | flops 4000000000 | bytes 4194304 | tf_op jit(solution)/shard_map/tile/pallas_call | solution.py:543
  68.1 2.9 %collective-permute-done.3 = bf16[8,32,256]{2,1,0:T(8,128)(2,1)S(1)} collective-permute-done((bf16[8,32,256]{2,1,0:T(8,128)(2,1)S(1)}, bf16[8,32,256]{2,1,0:T(8,128)(2,1)S(1)}, u32[]{:S(2)}, u32[]{:S(2)}) %collective-permute-start.3) | collective-permute-done | bytes 131104 | tf_op jit(solution)/shard_map/ppermute | solution.py:591
  71.0 1.7 %fusion = f32[8,256,256]{2,1,0:T(8,128)} fusion(f32[8,256,256]{2,1,0:T(8,128)} %tile.1, bf16[8,32,256]{2,1,0:T(8,128)(2,1)S(1)} %collective-permute-done.3), kind=kLoop, calls=%fused_computation.1 | loop fusion | flops 131072 | bytes 655360 | tf_op jit(solution)/shard_map/scatter-add | solution.py:594
Async XLA Ops:
  7.2 12.0 %collective-permute-start.1 = (bf16[8,64,128]{2,1,0:T(8,128)(2,1)}, bf16[8,64,128]{2,1,0:T(8,128)(2,1)S(1)}, u32[]{:S(2)}, u32[]{:S(2)}) collective-permute-start(bf16[8,64,128]{2,1,0:T(8,128)(2,1)} %get-tuple-element.25), channel_id=1, source_target_pairs={{0,16},{8,24},{16,0},{24,8},{1,17},{9,25},{17,1},{25,9},{2,18},{10... | collective-permute-start | bytes 393224 | tf_op jit(solution)/shard_map/ppermute | solution.py:578
  10.1 9.1 %collective-permute-start.2 = (bf16[8,64,128]{2,1,0:T(8,128)(2,1)}, bf16[8,64,128]{2,1,0:T(8,128)(2,1)S(1)}, u32[]{:S(2)}, u32[]{:S(2)}) collective-permute-start(bf16[8,64,128]{2,1,0:T(8,128)(2,1)} %get-tuple-element.26), channel_id=1, source_target_pairs={{0,24},{8,16},{16,8},{24,0},{1,25},{9,17},{17,9},{25,1},{2,26},{10... | collective-permute-start | bytes 393224 | tf_op jit(solution)/shard_map/ppermute | solution.py:578
  10.1 10.4 %copy-start.2 = (s32[1,1,32,1]{2,3,1,0:T(1,128)S(1)}, s32[1,1,32,1]{2,3,1,0:T(1,128)}, u32[]{:S(2)}) copy-start(s32[1,1,32,1]{2,3,1,0:T(1,128)} %param.25) | copy-start | bytes 388
  10.1 10.4 %copy-start.3 = (s32[1,1,32,1]{2,3,1,0:T(1,128)S(1)}, s32[1,1,32,1]{2,3,1,0:T(1,128)}, u32[]{:S(2)}) copy-start(s32[1,1,32,1]{2,3,1,0:T(1,128)} %param.26) | copy-start | bytes 388
  10.1 10.4 %copy-start.4 = (s32[1,1,32,1]{2,3,1,0:T(1,128)S(1)}, s32[1,1,32,1]{2,3,1,0:T(1,128)}, u32[]{:S(2)}) copy-start(s32[1,1,32,1]{2,3,1,0:T(1,128)} %param.27) | copy-start | bytes 388
  10.1 10.4 %copy-start.5 = (bf16[256,256]{1,0:T(8,128)(2,1)S(1)}, bf16[256,256]{1,0:T(8,128)(2,1)}, u32[]{:S(2)}) copy-start(bf16[256,256]{1,0:T(8,128)(2,1)} %constant.45.clone.w_low) | copy-start | bytes 393220
  10.1 10.4 %copy-start.6 = (bf16[256,256]{1,0:T(8,128)(2,1)S(1)}, bf16[256,256]{1,0:T(8,128)(2,1)}, u32[]{:S(2)}) copy-start(bf16[256,256]{1,0:T(8,128)(2,1)} %constant.44.clone.w_high) | copy-start | bytes 393220
  10.2 10.4 %copy-start.7 = (bf16[32,192]{1,0:T(8,128)(2,1)S(1)}, bf16[32,192]{1,0:T(8,128)(2,1)}, u32[]{:S(2)}) copy-start(bf16[32,192]{1,0:T(8,128)(2,1)} %constant.46.clone.f_rows) | copy-start | bytes 36868
  18.9 1.6 %collective-permute-start = (bf16[8,64,128]{2,1,0:T(8,128)(2,1)}, bf16[8,64,128]{2,1,0:T(8,128)(2,1)S(1)}, u32[]{:S(2)}, u32[]{:S(2)}) collective-permute-start(bf16[8,64,128]{2,1,0:T(8,128)(2,1)} %get-tuple-element.24), channel_id=1, source_target_pairs={{0,8},{8,0},{16,24},{24,16},{1,9},{9,1},{17,25},{25,17},{2,10},{10... | collective-permute-start | bytes 393224 | tf_op jit(solution)/shard_map/ppermute | solution.py:578
  20.6 1.2 %copy-start = (f32[2,32,32,128]{3,2,1,0:T(8,128)S(1)}, f32[2,32,32,128]{3,2,1,0:T(8,128)}, u32[]{:S(2)}) copy-start(f32[2,32,32,128]{3,2,1,0:T(8,128)} %get-tuple-element.22.gain) | copy-start | bytes 3145732
  21.8 0.9 %copy-start.1 = (bf16[8,64,128]{2,1,0:T(8,128)(2,1)S(1)}, bf16[8,64,128]{2,1,0:T(8,128)(2,1)}, u32[]{:S(2)}) copy-start(bf16[8,64,128]{2,1,0:T(8,128)(2,1)} %get-tuple-element.23.refs_0_) | copy-start | bytes 393220
  62.0 9.1 %collective-permute-start.3 = (bf16[8,32,256]{2,1,0:T(8,128)(2,1)S(1)}, bf16[8,32,256]{2,1,0:T(8,128)(2,1)S(1)}, u32[]{:S(2)}, u32[]{:S(2)}) collective-permute-start(bf16[8,32,256]{2,1,0:T(8,128)(2,1)S(1)} %margin.1), channel_id=1, source_target_pairs={{0,1},{1,2},{2,3},{3,4},{4,5},{5,6},{6,7},{7,8},{8,9},{9,10},{10,1... | collective-permute-start | bytes 393224 | tf_op jit(solution)/shard_map/ppermute | solution.py:591

commit v3 on v2

--- a/solution.py
+++ b/solution.py
@@ -317,7 +317,7 @@
         tiles = lane_tiles()
         operands = [stations] + operands + [aterm, taper, tiles]
         in_specs = [smem()] + in_specs + [
-            pl.BlockSpec(memory_space=pl.ANY),
+            pl.BlockSpec(memory_space=pltpu.HBM),
             pl.BlockSpec(taper.shape, lambda i, at: (0, 0)),
             pl.BlockSpec(tiles.shape, lambda i, at: (0, 0)),
         ]
@@ -334,7 +334,7 @@
             out_specs=out_specs,
             scratch_shapes=scratch,
         ),
-        compiler_params=pltpu.CompilerParams(vmem_limit_bytes=VMEM_LIMIT),
+        compiler_params=pltpu.CompilerParams(vmem_limit_bytes=(48 << 20) if gain_args else VMEM_LIMIT),
         cost_estimate=pl.CostEstimate(
             flops=len(ks) * count * FAN * 40000, bytes_accessed=1 << 20, transcendentals=0
         ),

time: 73.1 us -> 68.8 us (0.941)
  Pallas kernels: 24.8 us -> 22.7 us
  local copies, waits for them, and re-layouts: 2.16 us -> 0.07 us
    unnamed x16 -> x26, local copies, waits for them, and re-layouts: 2.16 us -> 0.07 us
    pallas_call x2, Pallas kernels: 15.3 us -> 13.6 us  [images(): pl.pallas_call(functools.partial(image_kernel, ks, bool(gain_args)), out_...]
  transfers between devices with their start and end apart: 4 -> 4, of which waited for: 2 -> 2; matrix products, arithmetic and copies ran while one was open for 0% -> 0% of each run, Pallas kernels for 20% -> 18%
where the time goes in v3:
time: 68.8 us
  blocking collectives  35.1 us (51%)
  Pallas kernels  22.7 us (33%)
  starting transfers between devices  4.54 us (7%)
  waiting for transfers between devices  3.84 us (6%)
  other arithmetic  1.68 us (2%)
  between operations  0.86 us (1%)
    all_to_all x1, blocking collectives, on_device(): lax.all_to_all(outgoing, ('freq', 'tile'), split_axis=0, concat_axis=0, t...  35.1 us
    pallas_call x2, Pallas kernels, images(): pl.pallas_call(functools.partial(image_kernel, ks, bool(gain_args)), out_...  13.6 us
    pallas_call x1, Pallas kernels, tile_of(): pl.pallas_call(tile_kernel, out_shape=jax.ShapeDtypeStruct((COMPS, TILE_W...  5.43 us
    ppermute x3, starting transfers between devices, make(): part = lax.ppermute(part, 'freq', [(i, i ^ k) for i in range(groups_n)])  3.14 us
    pallas_call x1, Pallas kernels, subgrids(): pl.pallas_call(functools.partial(subgrid_kernel, len(chunks)), out_shape=...  2.92 us
    ppermute x1, waiting for transfers between devices, on_device(): lax.ppermute(margin_of(arrived), ('freq', 'tile'), [(i, (i + 1) % devices...  2.62 us
    scatter-add x1, other arithmetic, on_device(): return tile_of(arrived).at[:, :SG, :].add(incoming.astype(f32))  1.68 us
    ppermute x1, starting transfers between devices, on_device(): lax.ppermute(margin_of(arrived), ('freq', 'tile'), [(i, (i + 1) % devices...  1.41 us
  transfers between devices with their start and end apart: 4, of which 2 were waited for; matrix products, arithmetic and copies ran while one was open for 0% of the time, Pallas kernels for 18%

profile of v3, /device:TPU:0, one launch (start us, length us, event | category | flops | bytes accessed | tf_op | source)
XLA Modules:
  0.0 68.8 jit_solution(10197602910809448218)
XLA Ops:
  0.7 0.0 copy-start
  0.7 0.0 copy-start.1
  0.7 0.0 copy-start.2
  0.7 0.0 copy-start.3
  0.7 0.0 copy-start.4
  0.7 0.0 copy-start.5
  0.7 0.0 copy-start.6
  0.7 6.6 %images.3 = (bf16[8,64,128]{2,1,0:T(8,128)(2,1)}, bf16[8,64,128]{2,1,0:T(8,128)(2,1)}) custom-call(s32[1]{0:T(128)} %bitcast.me, s32[1,1]{1,0:T(1,128)S(6)} %copy.18.valid, f32[64]{0:T(128)} %scales.3, bf16[8,64,1024]{2,1,0:T(8,128)(2,1)} %bitcast.6, f32[1,2,1024]{2,1,0:T(2,128)} %refs_1_.1, bf16[1024,256]{1,0:T(8,128)(2,1)} %constant.42.clone.refs_3_.refs_2_), custom_call_target="tpu_custom_call" | custom-call | flops 1310720000 | bytes 1048576 | tf_op jit(solution)/shard_map/images/pallas_call | solution.py:327
  7.4 2.9 %collective-permute-start.1 = (bf16[8,64,128]{2,1,0:T(8,128)(2,1)}, bf16[8,64,128]{2,1,0:T(8,128)(2,1)S(1)}, u32[]{:S(2)}, u32[]{:S(2)}) collective-permute-start(bf16[8,64,128]{2,1,0:T(8,128)(2,1)} %get-tuple-element.25), channel_id=1, source_target_pairs={{0,16},{8,24},{16,0},{24,8},{1,17},{9,25},{17,1},{25,9},{2,18},{10... | collective-permute-start | bytes 393224 | tf_op jit(solution)/shard_map/ppermute | solution.py:578
  10.3 0.0 collective-permute-start.2
  10.3 0.0 copy-done
  10.3 0.0 copy-done.1
  10.3 0.0 copy-done.2
  10.3 0.0 copy-done.3
  10.3 0.0 copy-done.4
  10.4 0.0 copy-done.5
  10.4 0.0 copy-done.6
  10.4 0.0 copy-start.7
  10.4 0.0 copy-start.8
  10.4 0.0 copy-start.9
  10.4 0.0 copy-start.10
  10.4 0.0 copy-start.11
  10.4 0.0 copy-start.12
  10.4 6.9 %images.2 = (bf16[8,64,128]{2,1,0:T(8,128)(2,1)S(1)}, bf16[8,64,128]{2,1,0:T(8,128)(2,1)S(1)}, f32[2,32,32,128]{3,2,1,0:T(8,128)S(1)}) custom-call(s32[1]{0:T(128)} %bitcast.me, s32[1,1]{1,0:T(1,128)S(6)} %copy.18.valid, f32[64]{0:T(128)S(1)} %copy-done.6, s32[1,1,2,32]{3,2,1,0:T(2,128)S(1)} %bitcast.8, bf16[8,64,1024]{2,1,0:T(8,128)(2,1)S(1)} %bitcast.7, ...), custom_call_target="tpu_custom_call" | custom-call | flops 1310720000 | bytes 1048576 | tf_op jit(solution)/shard_map/images/pallas_call | solution.py:327
  17.4 0.2 collective-permute-start
  17.6 0.0 collective-permute-done.1.refs_2_
  17.6 0.0 collective-permute-done.2.refs_3_
  17.6 1.2 %collective-permute-done.refs_1_ = bf16[8,64,128]{2,1,0:T(8,128)(2,1)S(1)} collective-permute-done((bf16[8,64,128]{2,1,0:T(8,128)(2,1)S(1)}, bf16[8,64,128]{2,1,0:T(8,128)(2,1)S(1)}, u32[]{:S(2)}, u32[]{:S(2)}) %collective-permute-start) | collective-permute-done | bytes 131104 | tf_op jit(solution)/shard_map/ppermute | solution.py:578
  18.8 0.0 copy-done.7
  18.8 0.0 copy-done.8
  18.8 0.0 copy-done.9
  18.8 0.0 copy-done.10
  18.8 0.0 copy-done.11
  18.8 0.0 copy-done.12
  18.8 2.9 %subgrids.1 = bf16[32,136,128]{2,1,0:T(8,128)(2,1)S(1)} custom-call(s32[1]{0:T(128)} %bitcast.me, s32[1,1,1,32]{3,2,1,0:T(1,128)S(1)} %bitcast.9, s32[1,1,1,32]{3,2,1,0:T(1,128)S(1)} %bitcast.10, s32[1,1,1,32]{3,2,1,0:T(1,128)S(1)} %bitcast.11, f32[2,32,32,128]{3,2,1,0:T(8,128)S(1)} %get-tuple-element.22.gain, bf16[256,256]{1,0:T(8,128)(2,1)S(1)} %copy-done.11, ...), custom_call_target="tpu_custom_call" | custom-call | flops 4000000000 | bytes 4194304 | tf_op jit(solution)/shard_map/subgrids/pallas_call | solution.py:409
  21.8 35.1 %all_to_all.5.arrived = bf16[32,136,128]{2,1,0:T(8,128)(2,1)S(1)} all-to-all(bf16[32,136,128]{2,1,0:T(8,128)(2,1)S(1)} %subgrids.1), channel_id=1, replica_groups=mesh['freq'=4,'tile'=8] {'freq','tile'}, dimensions={0} | all-to-all | bytes 2228224 | tf_op jit(solution)/shard_map/all_to_all | solution.py:588
  56.9 0.8 %margin.1 = bf16[8,32,256]{2,1,0:T(8,128)(2,1)S(1)} custom-call(bf16[32,136,128]{2,1,0:T(8,128)(2,1)S(1)} %all_to_all.5.arrived), custom_call_target="tpu_custom_call" | custom-call | tf_op jit(solution)/shard_map/margin/pallas_call | solution.py:485
  57.6 1.4 %collective-permute-start.3 = (bf16[8,32,256]{2,1,0:T(8,128)(2,1)S(1)}, bf16[8,32,256]{2,1,0:T(8,128)(2,1)S(1)}, u32[]{:S(2)}, u32[]{:S(2)}) collective-permute-start(bf16[8,32,256]{2,1,0:T(8,128)(2,1)S(1)} %margin.1), channel_id=1, source_target_pairs={{0,1},{1,2},{2,3},{3,4},{4,5},{5,6},{6,7},{7,8},{8,9},{9,10},{10,1... | collective-permute-start | bytes 393224 | tf_op jit(solution)/shard_map/ppermute | solution.py:591
  59.0 5.4 %tile.1 = f32[8,256,256]{2,1,0:T(8,128)} custom-call(bf16[32,136,128]{2,1,0:T(8,128)(2,1)S(1)} %all_to_all.5.arrived), custom_call_target="tpu_custom_call" | custom-call | flops 4000000000 | bytes 4194304 | tf_op jit(solution)/shard_map/tile/pallas_call | solution.py:543
  64.5 2.6 %collective-permute-done.3 = bf16[8,32,256]{2,1,0:T(8,128)(2,1)S(1)} collective-permute-done((bf16[8,32,256]{2,1,0:T(8,128)(2,1)S(1)}, bf16[8,32,256]{2,1,0:T(8,128)(2,1)S(1)}, u32[]{:S(2)}, u32[]{:S(2)}) %collective-permute-start.3) | collective-permute-done | bytes 131104 | tf_op jit(solution)/shard_map/ppermute | solution.py:591
  67.1 1.7 %fusion = f32[8,256,256]{2,1,0:T(8,128)} fusion(f32[8,256,256]{2,1,0:T(8,128)} %tile.1, bf16[8,32,256]{2,1,0:T(8,128)(2,1)S(1)} %collective-permute-done.3), kind=kLoop, calls=%fused_computation.1 | loop fusion | flops 131072 | bytes 655360 | tf_op jit(solution)/shard_map/scatter-add | solution.py:594
Async XLA Ops:
  0.7 9.7 %copy-start = (bf16[1,8,64,1024]{3,2,1,0:T(8,128)(2,1)S(1)}, bf16[1,8,64,1024]{3,2,1,0:T(8,128)(2,1)}, u32[]{:S(2)}) copy-start(bf16[1,8,64,1024]{3,2,1,0:T(8,128)(2,1)} %param.18) | copy-start | bytes 3145732
  0.7 9.7 %copy-start.1 = (bf16[1024,256]{1,0:T(8,128)(2,1)S(1)}, bf16[1024,256]{1,0:T(8,128)(2,1)}, u32[]{:S(2)}) copy-start(bf16[1024,256]{1,0:T(8,128)(2,1)} %constant.42.clone.refs_3_.refs_2_) | copy-start | bytes 1572868
  0.7 9.7 %copy-start.2 = (bf16[384,512]{1,0:T(8,128)(2,1)S(1)}, bf16[384,512]{1,0:T(8,128)(2,1)}, u32[]{:S(2)}) copy-start(bf16[384,512]{1,0:T(8,128)(2,1)} %constant.43.clone.refs_6_) | copy-start | bytes 1179652
  0.7 9.6 %copy-start.3 = (f32[32,32]{1,0:T(8,128)S(1)}, f32[32,32]{1,0:T(8,128)}, u32[]{:S(2)}) copy-start(f32[32,32]{1,0:T(8,128)} %refs_5_.1) | copy-start | bytes 12292
  0.7 9.6 %copy-start.4 = (f32[1,2,1024]{2,1,0:T(2,128)S(1)}, f32[1,2,1024]{2,1,0:T(2,128)}, u32[]{:S(2)}) copy-start(f32[1,2,1024]{2,1,0:T(2,128)} %refs_1_.1) | copy-start | bytes 24580
  0.7 9.6 %copy-start.5 = (s32[1,1,32,2]{2,3,1,0:T(2,128)S(1)}, s32[1,1,32,2]{2,3,1,0:T(2,128)}, u32[]{:S(2)}) copy-start(s32[1,1,32,2]{2,3,1,0:T(2,128)} %param.24) | copy-start | bytes 772
  0.7 9.6 %copy-start.6 = (f32[64]{0:T(128)S(1)}, f32[64]{0:T(128)}, u32[]{:S(2)}) copy-start(f32[64]{0:T(128)} %scales.3) | copy-start | bytes 772
  7.4 10.2 %collective-permute-start.1 = (bf16[8,64,128]{2,1,0:T(8,128)(2,1)}, bf16[8,64,128]{2,1,0:T(8,128)(2,1)S(1)}, u32[]{:S(2)}, u32[]{:S(2)}) collective-permute-start(bf16[8,64,128]{2,1,0:T(8,128)(2,1)} %get-tuple-element.25), channel_id=1, source_target_pairs={{0,16},{8,24},{16,0},{24,8},{1,17},{9,25},{17,1},{25,9},{2,18},{10... | collective-permute-start | bytes 393224 | tf_op jit(solution)/shard_map/ppermute | solution.py:578
  10.3 7.3 %collective-permute-start.2 = (bf16[8,64,128]{2,1,0:T(8,128)(2,1)}, bf16[8,64,128]{2,1,0:T(8,128)(2,1)S(1)}, u32[]{:S(2)}, u32[]{:S(2)}) collective-permute-start(bf16[8,64,128]{2,1,0:T(8,128)(2,1)} %get-tuple-element.26), channel_id=1, source_target_pairs={{0,24},{8,16},{16,8},{24,0},{1,25},{9,17},{17,9},{25,1},{2,26},{10... | collective-permute-start | bytes 393224 | tf_op jit(solution)/shard_map/ppermute | solution.py:578
  10.4 8.4 %copy-start.7 = (s32[1,1,32,1]{2,3,1,0:T(1,128)S(1)}, s32[1,1,32,1]{2,3,1,0:T(1,128)}, u32[]{:S(2)}) copy-start(s32[1,1,32,1]{2,3,1,0:T(1,128)} %param.25) | copy-start | bytes 388
  10.4 8.4 %copy-start.8 = (s32[1,1,32,1]{2,3,1,0:T(1,128)S(1)}, s32[1,1,32,1]{2,3,1,0:T(1,128)}, u32[]{:S(2)}) copy-start(s32[1,1,32,1]{2,3,1,0:T(1,128)} %param.26) | copy-start | bytes 388
  10.4 8.4 %copy-start.9 = (s32[1,1,32,1]{2,3,1,0:T(1,128)S(1)}, s32[1,1,32,1]{2,3,1,0:T(1,128)}, u32[]{:S(2)}) copy-start(s32[1,1,32,1]{2,3,1,0:T(1,128)} %param.27) | copy-start | bytes 388
  10.4 8.4 %copy-start.10 = (bf16[256,256]{1,0:T(8,128)(2,1)S(1)}, bf16[256,256]{1,0:T(8,128)(2,1)}, u32[]{:S(2)}) copy-start(bf16[256,256]{1,0:T(8,128)(2,1)} %constant.45.clone.w_low) | copy-start | bytes 393220
  10.4 8.4 %copy-start.11 = (bf16[256,256]{1,0:T(8,128)(2,1)S(1)}, bf16[256,256]{1,0:T(8,128)(2,1)}, u32[]{:S(2)}) copy-start(bf16[256,256]{1,0:T(8,128)(2,1)} %constant.44.clone.w_high) | copy-start | bytes 393220
  10.4 8.4 %copy-start.12 = (bf16[32,192]{1,0:T(8,128)(2,1)S(1)}, bf16[32,192]{1,0:T(8,128)(2,1)}, u32[]{:S(2)}) copy-start(bf16[32,192]{1,0:T(8,128)(2,1)} %constant.46.clone.f_rows) | copy-start | bytes 36868
  17.4 1.4 %collective-permute-start = (bf16[8,64,128]{2,1,0:T(8,128)(2,1)S(1)}, bf16[8,64,128]{2,1,0:T(8,128)(2,1)S(1)}, u32[]{:S(2)}, u32[]{:S(2)}) collective-permute-start(bf16[8,64,128]{2,1,0:T(8,128)(2,1)S(1)} %get-tuple-element.24), channel_id=1, source_target_pairs={{0,8},{8,0},{16,24},{24,16},{1,9},{9,1},{17,25},{25,17},{2,10},{10... | collective-permute-start | bytes 393224 | tf_op jit(solution)/shard_map/ppermute | solution.py:578
  57.6 9.5 %collective-permute-start.3 = (bf16[8,32,256]{2,1,0:T(8,128)(2,1)S(1)}, bf16[8,32,256]{2,1,0:T(8,128)(2,1)S(1)}, u32[]{:S(2)}, u32[]{:S(2)}) collective-permute-start(bf16[8,32,256]{2,1,0:T(8,128)(2,1)S(1)} %margin.1), channel_id=1, source_target_pairs={{0,1},{1,2},{2,3},{3,4},{4,5},{5,6},{6,7},{7,8},{8,9},{9,10},{10,1... | collective-permute-start | bytes 393224 | tf_op jit(solution)/shard_map/ppermute | solution.py:591

commit v4 on v3

--- a/solution.py
+++ b/solution.py
@@ -24,9 +24,9 @@
 NO_PLACE = 512.0
 COARSE = (4, 12)
 FINE = 4
-SUMS = 2 * (FINE + 1) * COMPS
+SUMS = 2 * FINE * COMPS
 CAP = 2
-U_STEP = SG + 3
+U_STEP = SG + 1
 V_STEP = 13
 W_STEP = CHAN_G + 1
 VMEM_LIMIT = 60 << 20
@@ -42,7 +42,7 @@
     return pl.BlockSpec(memory_space=pltpu.SMEM)
 
 
-IMAGE_ROWS = np.array([HALF + i for i in range(HALF)] + [0] + [HALF - i for i in range(1, HALF)])
+IMAGE_ROWS = np.array([HALF + i for i in range(HALF)] + [HALF - 1 - i for i in range(HALF)])
 
 
 def split(matrix):
@@ -80,23 +80,22 @@
 
 
 def combine_table():
-    table = np.zeros((4, 2, LANES, 2, 2, 2, SG))
+    table = np.zeros((4, 2, SUMS, 2, 2, 2, SG))
     for m in range(SG):
         for a, coarse in enumerate((COARSE[0], -COARSE[0], COARSE[1], -COARSE[1])):
-            b = m - HALF - coarse
-            if not -FINE <= b < FINE:
+            b = m - HALF + 0.5 - coarse
+            if abs(b) > FINE:
                 continue
-            size, sign = abs(b), 1 if b > 0 else -1
+            size, sign = int(abs(b)), 1 if b > 0 else -1
             for p in range(POL):
                 re, im = table[a, :, :, p // 2, p % 2, 0, m], table[a, :, :, p // 2, p % 2, 1, m]
-                at = 2 * FINE * COMPS if b == 0 else (size - 1) * COMPS
+                at = size * COMPS
                 re[0, at + p], im[0, at + POL + p] = 1, 1
                 re[1, at + POL + p], im[1, at + p] = -1, 1
-                if b:
-                    at += FINE * COMPS
-                    re[0, at + POL + p], im[0, at + p] = -sign, sign
-                    re[1, at + p], im[1, at + POL + p] = -sign, -sign
-    return table.reshape(8 * LANES, 2 * LANES).astype(ml_dtypes.bfloat16)
+                at += FINE * COMPS
+                re[0, at + POL + p], im[0, at + p] = -sign, sign
+                re[1, at + p], im[1, at + POL + p] = -sign, -sign
+    return table.reshape(4 * LANES, 2 * LANES).astype(ml_dtypes.bfloat16)
 
 
 def lane_tiles():
@@ -108,27 +107,32 @@
     return np.concatenate([table] * 3, 0).astype(ml_dtypes.bfloat16)
 
 
-def unit_powers(theta, wanted):
+def times(one, two):
+    return one[0] * two[0] - one[1] * two[1], one[0] * two[1] + one[1] * two[0]
+
+
+def squared(one):
+    return 1.0 - 2.0 * one[1] * one[1], 2.0 * one[1] * one[0]
+
+
+def half_angle(theta):
     half = theta * 0.5
     square = half * half
-    sin_h = half * (
+    sin = half * (
         1.0 + square * (-1.0 / 6 + square * (1.0 / 120 + square * (-1.0 / 5040 + square * (1.0 / 362880))))
     )
-    cos_h = 1.0 + square * (
+    cos = 1.0 + square * (
         -0.5 + square * (1.0 / 24 + square * (-1.0 / 720 + square * (1.0 / 40320 + square * (-1.0 / 3628800))))
     )
-    powers = {0: (jnp.ones_like(theta), jnp.zeros_like(theta))}
-    powers[1] = (1.0 - 2.0 * sin_h * sin_h, 2.0 * sin_h * cos_h)
-    for n in wanted:
-        if n in powers:
-            continue
-        first = n // 2 if n != 12 else 4
-        (ca, sa), (cb, sb) = powers[first], powers[n - first]
-        if 2 * first == n:
-            powers[n] = (1.0 - 2.0 * sa * sa, 2.0 * sa * ca)
-        else:
-            powers[n] = (ca * cb - sa * sb, ca * sb + sa * cb)
-    return powers
+    return cos, sin
+
+
+def odd_halves(half, count):
+    values, steps = [half], [squared(half)]
+    while len(values) < count:
+        values += [times(value, steps[-1]) for value in values]
+        steps.append(squared(steps[-1]))
+    return values, steps
 
 
 def gain_copies(stations, aterm, rows, sems):
@@ -189,31 +193,34 @@
             copy.start()
 
     lane = lax.broadcasted_iota(jnp.int32, (CHAN_G, TSTEP), 1)
-    first_row = lax.broadcasted_iota(jnp.int32, (HALF, LANES), 0) == 0
 
     def build(s, scale):
         u_tab, v_tab, w_tab = u_tabs.at[s % 2], v_tabs.at[s % 2], w_tabs.at[s % 2]
         part = pl.ds(s * TSTEP, TSTEP)
         live = lane + s * TSTEP < valid[0, 0]
+        parts = []
         for c in range(COMPS):
             values = vis_ref[c, :, part].astype(f32)
-            w_tab[pl.ds(c * W_STEP, CHAN_G), :] = jnp.where(live, values, 0.0)
-        powers = unit_powers(uv_ref[0, 0:1, part] * scale, range(HALF + 1))
-        for n in range(HALF):
-            u_tab[pl.ds(n, CHAN_G, U_STEP), :] = powers[n][0]
-            u_tab[pl.ds(HALF + n, CHAN_G, U_STEP), :] = powers[n][1]
-        u_tab[pl.ds(SG, CHAN_G, U_STEP), :] = powers[HALF][0]
-        u_tab[pl.ds(SG + 1, CHAN_G, U_STEP), :] = powers[HALF][1]
-        powers = unit_powers(uv_ref[0, 1:2, part] * scale, (1, 2, 3, 4, 8, 12))
-        for q, n in enumerate(COARSE):
-            v_tab[pl.ds(2 * q, CHAN_G, V_STEP), :] = powers[n][0]
-            v_tab[pl.ds(2 * q + 1, CHAN_G, V_STEP), :] = powers[n][1]
-        for n in range(1, FINE + 1):
-            v_tab[pl.ds(3 + n, CHAN_G, V_STEP), :] = powers[n][0]
-            v_tab[pl.ds(3 + FINE + n, CHAN_G, V_STEP), :] = powers[n][1]
+            parts.append(jnp.where(live, values, 0.0))
+        u_half = half_angle(uv_ref[0, 0:1, part] * scale)
+        v_half = half_angle(uv_ref[0, 1:2, part] * scale)
+        cos, sin = times(u_half, v_half)
+        for p in range(POL):
+            re, im = parts[p], parts[POL + p]
+            w_tab[pl.ds(p * W_STEP, CHAN_G), :] = re * cos + im * sin
+            w_tab[pl.ds((POL + p) * W_STEP, CHAN_G), :] = im * cos - re * sin
+        for n, value in enumerate(odd_halves(u_half, HALF)[0]):
+            u_tab[pl.ds(n, CHAN_G, U_STEP), :] = value[0]
+            u_tab[pl.ds(HALF + n, CHAN_G, U_STEP), :] = value[1]
+        values, steps = odd_halves(v_half, FINE)
+        for n, value in enumerate(values):
+            v_tab[pl.ds(4 + n, CHAN_G, V_STEP), :] = value[0]
+            v_tab[pl.ds(4 + FINE + n, CHAN_G, V_STEP), :] = value[1]
+        for q, value in enumerate((steps[-1], times(steps[-1], squared(steps[-1])))):
+            v_tab[pl.ds(2 * q, CHAN_G, V_STEP), :] = value[0]
+            v_tab[pl.ds(2 * q + 1, CHAN_G, V_STEP), :] = value[1]
         sums = None
         step = 4
-        pad = jnp.zeros((COMPS, TSTEP), f32)
         for start in range(0, CHAN_G, step):
             left, right = [], []
             for h in range(start, start + step):
@@ -221,13 +228,10 @@
                 column = [
                     (u_rows * v_tab[pl.ds(h * V_STEP + a, 1), :]).astype(bf16) for a in range(4)
                 ]
-                coarse = v_tab[pl.ds(h * V_STEP, 4), :]
-                last = [coarse * u_tab[pl.ds(h * U_STEP + SG + i, 1), :] for i in range(2)]
-                column.append(jnp.concatenate(last + [pad], 0).astype(bf16))
                 left.append(jnp.concatenate(column, 0))
                 w_all = w_tab[pl.ds(h, COMPS, W_STEP), :]
                 fine = [w_all * v_tab[pl.ds(h * V_STEP + 4 + b, 1), :] for b in range(2 * FINE)]
-                right.append(jnp.concatenate(fine + [w_all, pad], 0).astype(bf16))
+                right.append(jnp.concatenate(fine, 0).astype(bf16))
             term = lax.dot_general(
                 jnp.concatenate(left, 1),
                 jnp.concatenate(right, 1),
@@ -238,25 +242,17 @@
         return sums
 
     def keep(s, sums):
-        top = 4 * SG
-        sums = jnp.concatenate([sums, jnp.zeros((sums.shape[0], LANES - SUMS), f32)], 1)
         for q in range(2):
             cos, sin = sums[2 * q * SG : (2 * q + 1) * SG], sums[(2 * q + 1) * SG : (2 * q + 2) * SG]
             cc, sc, cs, ss = cos[:HALF], cos[HALF:], sin[:HALF], sin[HALF:]
-            ends = [sums[top + e : top + e + 1] for e in (2 * q, 4 + 2 * q, 2 * q + 1, 5 + 2 * q)]
-            ecc, esc, ecs, ess = [jnp.where(first_row, e, x) for e, x in zip(ends, (cc, sc, cs, ss))]
             for d, (zero, one) in enumerate(
-                (
-                    ((cc - ss, ecc + ess), (sc + cs, ecs - esc)),
-                    ((cc + ss, ecc - ess), (sc - cs, -esc - ecs)),
-                )
+                (((cc - ss, cc + ss), (sc + cs, cs - sc)), ((cc + ss, cc - ss), (sc - cs, -sc - cs)))
             ):
-                for x, values in enumerate((zero, one)):
-                    both = jnp.concatenate(values, 0)
-                    high = both.astype(bf16)
-                    at = ((2 * q + d) * 2 + x) * LANES
-                    x_high[s * SG : (s + 1) * SG, at : at + LANES] = high
-                    x_low[s * SG : (s + 1) * SG, at : at + LANES] = (both - high.astype(f32)).astype(bf16)
+                both = jnp.concatenate([jnp.concatenate(zero, 0), jnp.concatenate(one, 0)], 1)
+                high = both.astype(bf16)
+                at = (2 * q + d) * LANES
+                x_high[s * SG : (s + 1) * SG, at : at + LANES] = high
+                x_low[s * SG : (s + 1) * SG, at : at + LANES] = (both - high.astype(f32)).astype(bf16)
 
     group = me[0] ^ (ks[0] - turn)
     for h in range(CHAN_G):
@@ -307,8 +303,8 @@
         pltpu.VMEM((2, CHAN_G * V_STEP, LANES), f32),
         pltpu.VMEM((2, COMPS * W_STEP, LANES), f32),
         pltpu.VMEM((CHAN_G, LANES), f32),
-        pltpu.VMEM((count * SG, 8 * LANES), bf16),
-        pltpu.VMEM((count * SG, 8 * LANES), bf16),
+        pltpu.VMEM((count * SG, 4 * LANES), bf16),
+        pltpu.VMEM((count * SG, 4 * LANES), bf16),
     ]
     operands = [vis, uv, table]
     if gain_args:
@@ -498,7 +494,7 @@
     )(arrived)
 
 
-def tile_kernel(arrived, out_ref, columns, spread, places, result, sems):
+def tile_kernel(arrived, out_ref, head_ref, columns, spread, places, result, sems):
     sources = arrived.shape[0]
     per_lanes = LANES // SG
     places[...] = arrived[:, CAP * 2 * SG :, :].astype(f32)
@@ -532,7 +528,11 @@
         result[comp] = jnp.dot(
             columns[...], spread[:, comp * BAND_V : (comp + 1) * BAND_V], preferred_element_type=f32
         )
-        copies.append(pltpu.make_async_copy(result.at[comp], out_ref.at[comp], sems.at[comp]))
+        head_ref[comp] = result[comp, :SG, :]
+        rest = pl.ds(SG, TILE_W - SG)
+        copies.append(
+            pltpu.make_async_copy(result.at[comp, rest], out_ref.at[comp, rest], sems.at[comp])
+        )
         copies[-1].start()
     for copy in copies:
         copy.wait()
@@ -542,9 +542,12 @@
     cells = arrived.shape[0] * CAP * SG
     return pl.pallas_call(
         tile_kernel,
-        out_shape=jax.ShapeDtypeStruct((COMPS, TILE_W, BAND_V), f32),
+        out_shape=(
+            jax.ShapeDtypeStruct((COMPS, TILE_W, BAND_V), f32),
+            jax.ShapeDtypeStruct((COMPS, SG, BAND_V), f32),
+        ),
         in_specs=[vmem()],
-        out_specs=pl.BlockSpec(memory_space=pl.ANY),
+        out_specs=(pl.BlockSpec(memory_space=pl.ANY), vmem()),
         scratch_shapes=[
             pltpu.VMEM((TILE_W, cells), bf16),
             pltpu.VMEM((cells, COMPS * BAND_V), bf16),
@@ -591,7 +594,8 @@
     incoming = lax.ppermute(
         margin_of(arrived), ("freq", "tile"), [(i, (i + 1) % devices_n) for i in range(devices_n)]
     )
-    return tile_of(arrived).at[:, :SG, :].add(incoming.astype(f32))
+    tile, head = tile_of(arrived)
+    return tile.at[:, :SG, :].set(head + incoming.astype(f32))
 
 
 def solution(mesh):

time: 68.8 us -> 67.4 us (0.980)
  other arithmetic: 1.68 us -> 0.73 us
    scatter-add x1 -> x0, other arithmetic: 1.68 us -> none  [on_device(): return tile_of(arrived).at[:, :SG, :].add(incoming.astype(f32))]
    pallas_call x2, Pallas kernels: 13.6 us -> 12.8 us  [images(): pl.pallas_call(functools.partial(image_kernel, ks, bool(gain_args)), out_...]
    scatter x0 -> x1, other arithmetic: none -> 0.73 us  [on_device(): return tile.at[:, :SG, :].set(head + incoming.astype(f32))]
where the time goes in v4:
time: 67.4 us
  blocking collectives  35.1 us (52%)
  Pallas kernels  22.2 us (33%)
  waiting for transfers between devices  4.2 us (6%)
  starting transfers between devices  4.19 us (6%)
  between operations  0.86 us (1%)
  other arithmetic  0.73 us (1%)
    all_to_all x1, blocking collectives, on_device(): lax.all_to_all(outgoing, ('freq', 'tile'), split_axis=0, concat_axis=0, t...  35.1 us
    pallas_call x2, Pallas kernels, images(): pl.pallas_call(functools.partial(image_kernel, ks, bool(gain_args)), out_...  12.8 us
    pallas_call x1, Pallas kernels, tile_of(): pl.pallas_call(tile_kernel, out_shape=(jax.ShapeDtypeStruct((COMPS, TILE_...  5.42 us
    ppermute x3, starting transfers between devices, make(): part = lax.ppermute(part, 'freq', [(i, i ^ k) for i in range(groups_n)])  3.14 us
    ppermute x1, waiting for transfers between devices, on_device(): lax.ppermute(margin_of(arrived), ('freq', 'tile'), [(i, (i + 1) % devices...  2.99 us
    pallas_call x1, Pallas kernels, subgrids(): pl.pallas_call(functools.partial(subgrid_kernel, len(chunks)), out_shape=...  2.92 us
  transfers between devices with their start and end apart: 4, of which 2 were waited for; matrix products, arithmetic and copies ran while one was open for 0% of the time, Pallas kernels for 18%

profile of v4, /device:TPU:0, one launch (start us, length us, event | category | flops | bytes accessed | tf_op | source)
XLA Modules:
  0.0 67.4 jit_solution(5608174325424890626)
XLA Ops:
  0.7 0.0 copy-start
  0.7 0.0 copy-start.1
  0.7 0.0 copy-start.2
  0.7 0.0 copy-start.3
  0.7 0.0 copy-start.4
  0.7 0.0 copy-start.5
  0.7 0.0 copy-start.6
  0.7 6.2 %images.3 = (bf16[8,64,128]{2,1,0:T(8,128)(2,1)}, bf16[8,64,128]{2,1,0:T(8,128)(2,1)}) custom-call(s32[1]{0:T(128)} %bitcast.me, s32[1,1]{1,0:T(1,128)S(6)} %copy.18.valid, f32[64]{0:T(128)} %scales.3, bf16[8,64,1024]{2,1,0:T(8,128)(2,1)} %bitcast.6, f32[1,2,1024]{2,1,0:T(2,128)} %refs_1_.1, bf16[512,256]{1,0:T(8,128)(2,1)} %constant.42.clone.refs_3_.refs_2_), custom_call_target="tpu_custom_call" | custom-call | flops 1310720000 | bytes 1048576 | tf_op jit(solution)/shard_map/images/pallas_call | solution.py:323
  6.9 2.9 %collective-permute-start.1 = (bf16[8,64,128]{2,1,0:T(8,128)(2,1)}, bf16[8,64,128]{2,1,0:T(8,128)(2,1)S(1)}, u32[]{:S(2)}, u32[]{:S(2)}) collective-permute-start(bf16[8,64,128]{2,1,0:T(8,128)(2,1)} %get-tuple-element.27), channel_id=1, source_target_pairs={{0,16},{8,24},{16,0},{24,8},{1,17},{9,25},{17,1},{25,9},{2,18},{10... | collective-permute-start | bytes 393224 | tf_op jit(solution)/shard_map/ppermute | solution.py:581
  9.9 0.0 collective-permute-start.2
  9.9 0.0 copy-done
  9.9 0.0 copy-done.1
  9.9 0.0 copy-done.2
  9.9 0.0 copy-done.3
  9.9 0.0 copy-done.4
  9.9 0.0 copy-done.5
  9.9 0.0 copy-done.6
  9.9 0.0 copy-start.7
  9.9 0.0 copy-start.8
  9.9 0.0 copy-start.9
  9.9 0.0 copy-start.10
  10.0 0.0 copy-start.11
  10.0 0.0 copy-start.12
  10.0 6.6 %images.2 = (bf16[8,64,128]{2,1,0:T(8,128)(2,1)S(1)}, bf16[8,64,128]{2,1,0:T(8,128)(2,1)S(1)}, f32[2,32,32,128]{3,2,1,0:T(8,128)S(1)}) custom-call(s32[1]{0:T(128)} %bitcast.me, s32[1,1]{1,0:T(1,128)S(6)} %copy.18.valid, f32[64]{0:T(128)S(1)} %copy-done.6, s32[1,1,2,32]{3,2,1,0:T(2,128)S(1)} %bitcast.8, bf16[8,64,1024]{2,1,0:T(8,128)(2,1)S(1)} %bitcast.7, ...), custom_call_target="tpu_custom_call" | custom-call | flops 1310720000 | bytes 1048576 | tf_op jit(solution)/shard_map/images/pallas_call | solution.py:323
  16.6 0.2 collective-permute-start
  16.8 0.0 collective-permute-done.1.refs_2_
  16.8 0.0 collective-permute-done.2.refs_3_
  16.8 1.2 %collective-permute-done.refs_1_ = bf16[8,64,128]{2,1,0:T(8,128)(2,1)S(1)} collective-permute-done((bf16[8,64,128]{2,1,0:T(8,128)(2,1)S(1)}, bf16[8,64,128]{2,1,0:T(8,128)(2,1)S(1)}, u32[]{:S(2)}, u32[]{:S(2)}) %collective-permute-start) | collective-permute-done | bytes 131104 | tf_op jit(solution)/shard_map/ppermute | solution.py:581
  18.0 0.0 copy-done.7
  18.0 0.0 copy-done.8
  18.0 0.0 copy-done.9
  18.0 0.0 copy-done.10
  18.0 0.0 copy-done.11
  18.0 0.0 copy-done.12
  18.0 2.9 %subgrids.1 = bf16[32,136,128]{2,1,0:T(8,128)(2,1)S(1)} custom-call(s32[1]{0:T(128)} %bitcast.me, s32[1,1,1,32]{3,2,1,0:T(1,128)S(1)} %bitcast.9, s32[1,1,1,32]{3,2,1,0:T(1,128)S(1)} %bitcast.10, s32[1,1,1,32]{3,2,1,0:T(1,128)S(1)} %bitcast.11, f32[2,32,32,128]{3,2,1,0:T(8,128)S(1)} %get-tuple-element.24.gain, bf16[256,256]{1,0:T(8,128)(2,1)S(1)} %copy-done.11, ...), custom_call_target="tpu_custom_call" | custom-call | flops 4000000000 | bytes 4194304 | tf_op jit(solution)/shard_map/subgrids/pallas_call | solution.py:405
  21.0 35.1 %all_to_all.5.arrived = bf16[32,136,128]{2,1,0:T(8,128)(2,1)S(1)} all-to-all(bf16[32,136,128]{2,1,0:T(8,128)(2,1)S(1)} %subgrids.1), channel_id=1, replica_groups=mesh['freq'=4,'tile'=8] {'freq','tile'}, dimensions={0} | all-to-all | bytes 2228224 | tf_op jit(solution)/shard_map/all_to_all | solution.py:591
  56.1 1.1 %margin.1 = bf16[8,32,256]{2,1,0:T(8,128)(2,1)S(1)} custom-call(bf16[32,136,128]{2,1,0:T(8,128)(2,1)S(1)} %all_to_all.5.arrived), custom_call_target="tpu_custom_call" | custom-call | tf_op jit(solution)/shard_map/margin/pallas_call | solution.py:481
  57.2 1.1 %collective-permute-start.3 = (bf16[8,32,256]{2,1,0:T(8,128)(2,1)S(1)}, bf16[8,32,256]{2,1,0:T(8,128)(2,1)S(1)}, u32[]{:S(2)}, u32[]{:S(2)}) collective-permute-start(bf16[8,32,256]{2,1,0:T(8,128)(2,1)S(1)} %margin.1), channel_id=1, source_target_pairs={{0,1},{1,2},{2,3},{3,4},{4,5},{5,6},{6,7},{7,8},{8,9},{9,10},{10,1... | collective-permute-start | bytes 393224 | tf_op jit(solution)/shard_map/ppermute | solution.py:594
  58.3 5.4 %tile.1 = (f32[8,256,256]{2,1,0:T(8,128)}, f32[8,32,256]{2,1,0:T(8,128)S(1)}) custom-call(bf16[32,136,128]{2,1,0:T(8,128)(2,1)S(1)} %all_to_all.5.arrived), custom_call_target="tpu_custom_call" | custom-call | flops 4000000000 | bytes 4194304 | tf_op jit(solution)/shard_map/tile/pallas_call | solution.py:543
  63.7 3.0 %collective-permute-done.3 = bf16[8,32,256]{2,1,0:T(8,128)(2,1)S(1)} collective-permute-done((bf16[8,32,256]{2,1,0:T(8,128)(2,1)S(1)}, bf16[8,32,256]{2,1,0:T(8,128)(2,1)S(1)}, u32[]{:S(2)}, u32[]{:S(2)}) %collective-permute-start.3) | collective-permute-done | bytes 131104 | tf_op jit(solution)/shard_map/ppermute | solution.py:594
  66.7 0.7 %add_dynamic-update-slice_fusion = f32[8,256,256]{2,1,0:T(8,128)} fusion(f32[8,256,256]{2,1,0:T(8,128)} %get-tuple-element.29, f32[8,32,256]{2,1,0:T(8,128)S(1)} %get-tuple-element.30, bf16[8,32,256]{2,1,0:T(8,128)(2,1)S(1)} %collective-permute-done.3), kind=kLoop, calls=%fused_computation | loop fusion | flops 131072 | bytes 655360 | tf_op jit(solution)/shard_map/scatter | solution.py:598
Async XLA Ops:
  0.7 9.2 %copy-start = (bf16[1,8,64,1024]{3,2,1,0:T(8,128)(2,1)S(1)}, bf16[1,8,64,1024]{3,2,1,0:T(8,128)(2,1)}, u32[]{:S(2)}) copy-start(bf16[1,8,64,1024]{3,2,1,0:T(8,128)(2,1)} %param.18) | copy-start | bytes 3145732
  0.7 9.2 %copy-start.1 = (bf16[384,512]{1,0:T(8,128)(2,1)S(1)}, bf16[384,512]{1,0:T(8,128)(2,1)}, u32[]{:S(2)}) copy-start(bf16[384,512]{1,0:T(8,128)(2,1)} %constant.43.clone.refs_6_) | copy-start | bytes 1179652
  0.7 9.2 %copy-start.2 = (bf16[512,256]{1,0:T(8,128)(2,1)S(1)}, bf16[512,256]{1,0:T(8,128)(2,1)}, u32[]{:S(2)}) copy-start(bf16[512,256]{1,0:T(8,128)(2,1)} %constant.42.clone.refs_3_.refs_2_) | copy-start | bytes 786436
  0.7 9.2 %copy-start.3 = (f32[32,32]{1,0:T(8,128)S(1)}, f32[32,32]{1,0:T(8,128)}, u32[]{:S(2)}) copy-start(f32[32,32]{1,0:T(8,128)} %refs_5_.1) | copy-start | bytes 12292
  0.7 9.2 %copy-start.4 = (f32[1,2,1024]{2,1,0:T(2,128)S(1)}, f32[1,2,1024]{2,1,0:T(2,128)}, u32[]{:S(2)}) copy-start(f32[1,2,1024]{2,1,0:T(2,128)} %refs_1_.1) | copy-start | bytes 24580
  0.7 9.2 %copy-start.5 = (s32[1,1,32,2]{2,3,1,0:T(2,128)S(1)}, s32[1,1,32,2]{2,3,1,0:T(2,128)}, u32[]{:S(2)}) copy-start(s32[1,1,32,2]{2,3,1,0:T(2,128)} %param.24) | copy-start | bytes 772
  0.7 9.2 %copy-start.6 = (f32[64]{0:T(128)S(1)}, f32[64]{0:T(128)}, u32[]{:S(2)}) copy-start(f32[64]{0:T(128)} %scales.3) | copy-start | bytes 772
  6.9 9.9 %collective-permute-start.1 = (bf16[8,64,128]{2,1,0:T(8,128)(2,1)}, bf16[8,64,128]{2,1,0:T(8,128)(2,1)S(1)}, u32[]{:S(2)}, u32[]{:S(2)}) collective-permute-start(bf16[8,64,128]{2,1,0:T(8,128)(2,1)} %get-tuple-element.27), channel_id=1, source_target_pairs={{0,16},{8,24},{16,0},{24,8},{1,17},{9,25},{17,1},{25,9},{2,18},{10... | collective-permute-start | bytes 393224 | tf_op jit(solution)/shard_map/ppermute | solution.py:581
  9.9 6.9 %collective-permute-start.2 = (bf16[8,64,128]{2,1,0:T(8,128)(2,1)}, bf16[8,64,128]{2,1,0:T(8,128)(2,1)S(1)}, u32[]{:S(2)}, u32[]{:S(2)}) collective-permute-start(bf16[8,64,128]{2,1,0:T(8,128)(2,1)} %get-tuple-element.28), channel_id=1, source_target_pairs={{0,24},{8,16},{16,8},{24,0},{1,25},{9,17},{17,9},{25,1},{2,26},{10... | collective-permute-start | bytes 393224 | tf_op jit(solution)/shard_map/ppermute | solution.py:581
  9.9 8.1 %copy-start.7 = (s32[1,1,32,1]{2,3,1,0:T(1,128)S(1)}, s32[1,1,32,1]{2,3,1,0:T(1,128)}, u32[]{:S(2)}) copy-start(s32[1,1,32,1]{2,3,1,0:T(1,128)} %param.25) | copy-start | bytes 388
  9.9 8.1 %copy-start.8 = (s32[1,1,32,1]{2,3,1,0:T(1,128)S(1)}, s32[1,1,32,1]{2,3,1,0:T(1,128)}, u32[]{:S(2)}) copy-start(s32[1,1,32,1]{2,3,1,0:T(1,128)} %param.26) | copy-start | bytes 388
  9.9 8.1 %copy-start.9 = (s32[1,1,32,1]{2,3,1,0:T(1,128)S(1)}, s32[1,1,32,1]{2,3,1,0:T(1,128)}, u32[]{:S(2)}) copy-start(s32[1,1,32,1]{2,3,1,0:T(1,128)} %param.27) | copy-start | bytes 388
  9.9 8.1 %copy-start.10 = (bf16[256,256]{1,0:T(8,128)(2,1)S(1)}, bf16[256,256]{1,0:T(8,128)(2,1)}, u32[]{:S(2)}) copy-start(bf16[256,256]{1,0:T(8,128)(2,1)} %constant.45.clone.w_low) | copy-start | bytes 393220
  10.0 8.1 %copy-start.11 = (bf16[256,256]{1,0:T(8,128)(2,1)S(1)}, bf16[256,256]{1,0:T(8,128)(2,1)}, u32[]{:S(2)}) copy-start(bf16[256,256]{1,0:T(8,128)(2,1)} %constant.44.clone.w_high) | copy-start | bytes 393220
  10.0 8.1 %copy-start.12 = (bf16[32,192]{1,0:T(8,128)(2,1)S(1)}, bf16[32,192]{1,0:T(8,128)(2,1)}, u32[]{:S(2)}) copy-start(bf16[32,192]{1,0:T(8,128)(2,1)} %constant.46.clone.f_rows) | copy-start | bytes 36868
  16.6 1.4 %collective-permute-start = (bf16[8,64,128]{2,1,0:T(8,128)(2,1)S(1)}, bf16[8,64,128]{2,1,0:T(8,128)(2,1)S(1)}, u32[]{:S(2)}, u32[]{:S(2)}) collective-permute-start(bf16[8,64,128]{2,1,0:T(8,128)(2,1)S(1)} %get-tuple-element.26), channel_id=1, source_target_pairs={{0,8},{8,0},{16,24},{24,16},{1,9},{9,1},{17,25},{25,17},{2,10},{10... | collective-permute-start | bytes 393224 | tf_op jit(solution)/shard_map/ppermute | solution.py:581
  57.2 9.5 %collective-permute-start.3 = (bf16[8,32,256]{2,1,0:T(8,128)(2,1)S(1)}, bf16[8,32,256]{2,1,0:T(8,128)(2,1)S(1)}, u32[]{:S(2)}, u32[]{:S(2)}) collective-permute-start(bf16[8,32,256]{2,1,0:T(8,128)(2,1)S(1)} %margin.1), channel_id=1, source_target_pairs={{0,1},{1,2},{2,3},{3,4},{4,5},{5,6},{6,7},{7,8},{8,9},{9,10},{10,1... | collective-permute-start | bytes 393224 | tf_op jit(solution)/shard_map/ppermute | solution.py:594

commit v5 on v4

--- a/solution.py
+++ b/solution.py
@@ -342,7 +342,7 @@
     chunks = refs[:chunks_n]
     out_ref, d_high, d_low, y_ref, pos, taken = refs[chunks_n:]
     block = chunks[0].shape[0]
-    row = lax.broadcasted_iota(jnp.int32, (POS_ROWS, LANES), 0)
+    row = lax.broadcasted_iota(jnp.int32, (2, LANES), 0)
 
     def clear(i, _):
         taken[i] = 0
@@ -362,14 +362,14 @@
                 at = pl.ds(((k * block + i) * 2 + pair) * SG, SG)
                 d_high[at, :] = high
                 d_low[at, :] = (both - high.astype(f32)).astype(bf16)
-    step = 256
+    step = 128
     for i in range(d_high.shape[0] // step):
         at = pl.ds(i * step, step)
         high = d_high[at, :]
-        y_ref[at, :] = (
-            jnp.dot(high, w_high[...], preferred_element_type=f32)
-            + jnp.dot(d_low[at, :], w_high[...], preferred_element_type=f32)
-            + jnp.dot(high, w_low[...], preferred_element_type=f32)
+        y_ref[at, :] = jnp.dot(
+            jnp.concatenate([high, d_low[at, :], high], 1),
+            jnp.concatenate([w_high[...], w_high[...], w_low[...]], 0),
+            preferred_element_type=f32,
         )
     for k in range(chunks_n):
         base = (me[0] ^ k) * block
@@ -396,7 +396,7 @@
                 start = pl.multiple_of((slot * 2 + pair) * SG, SG)
                 out_ref[dest, pl.ds(start, SG), :] = cells[:, pair * LANES : (pair + 1) * LANES]
             u, v = u_offset[0, 0, 0, s].astype(f32), v_start[0, 0, 0, s].astype(f32)
-            pos[dest] = jnp.where(row == 2 * slot, u, jnp.where(row == 2 * slot + 1, v, pos[dest]))
+            pos[dest, pl.ds(2 * slot, 2), :] = jnp.where(row == 0, u, v)
     out_ref[:, CAP * 2 * SG :, :] = pos[...].astype(bf16)
 
 

time: 67.4 us -> 67 us (level)
  no operation moved by 1% of the time
where the time goes in v5:
time: 67 us; the launch traced here: 66.9 us
  blocking collectives  35.1 us (52%)
  Pallas kernels  21.7 us (32%)
  starting transfers between devices  4.2 us (6%)
  waiting for transfers between devices  4.19 us (6%)
  between operations  0.86 us (1%)
  other arithmetic  0.73 us (1%)
    all_to_all x1, blocking collectives, on_device(): lax.all_to_all(outgoing, ('freq', 'tile'), split_axis=0, concat_axis=0, t...  35.1 us
    pallas_call x2, Pallas kernels, images(): pl.pallas_call(functools.partial(image_kernel, ks, bool(gain_args)), out_...  12.8 us
    pallas_call x1, Pallas kernels, tile_of(): pl.pallas_call(tile_kernel, out_shape=(jax.ShapeDtypeStruct((COMPS, TILE_...  5.43 us
    ppermute x3, starting transfers between devices, make(): part = lax.ppermute(part, 'freq', [(i, i ^ k) for i in range(groups_n)])  3.14 us
    ppermute x1, waiting for transfers between devices, on_device(): lax.ppermute(margin_of(arrived), ('freq', 'tile'), [(i, (i + 1) % devices...  2.98 us
    pallas_call x1, Pallas kernels, subgrids(): pl.pallas_call(functools.partial(subgrid_kernel, len(chunks)), out_shape=...  2.77 us
  transfers between devices with their start and end apart: 4, of which 2 were waited for; matrix products, arithmetic and copies ran while one was open for 0% of the time, Pallas kernels for 18%

profile of v5, /device:TPU:0, one launch (start us, length us, event | category | flops | bytes accessed | tf_op | source)
XLA Modules:
  0.0 66.9 jit_solution(2818897603539622974)
XLA Ops:
  0.7 0.0 copy-start
  0.7 0.0 copy-start.1
  0.7 0.0 copy-start.2
  0.7 0.0 copy-start.3
  0.7 0.0 copy-start.4
  0.7 0.0 copy-start.5
  0.7 0.0 copy-start.6
  0.7 6.2 %images.3 = (bf16[8,64,128]{2,1,0:T(8,128)(2,1)}, bf16[8,64,128]{2,1,0:T(8,128)(2,1)}) custom-call(s32[1]{0:T(128)} %bitcast.me, s32[1,1]{1,0:T(1,128)S(6)} %copy.18.valid, f32[64]{0:T(128)} %scales.3, bf16[8,64,1024]{2,1,0:T(8,128)(2,1)} %bitcast.6, f32[1,2,1024]{2,1,0:T(2,128)} %refs_1_.1, bf16[512,256]{1,0:T(8,128)(2,1)} %constant.42.clone.refs_3_.refs_2_), custom_call_target="tpu_custom_call" | custom-call | flops 1310720000 | bytes 1048576 | tf_op jit(solution)/shard_map/images/pallas_call | solution.py:323
  6.9 2.9 %collective-permute-start.1 = (bf16[8,64,128]{2,1,0:T(8,128)(2,1)}, bf16[8,64,128]{2,1,0:T(8,128)(2,1)S(1)}, u32[]{:S(2)}, u32[]{:S(2)}) collective-permute-start(bf16[8,64,128]{2,1,0:T(8,128)(2,1)} %get-tuple-element.27), channel_id=1, source_target_pairs={{0,16},{8,24},{16,0},{24,8},{1,17},{9,25},{17,1},{25,9},{2,18},{10... | collective-permute-start | bytes 393224 | tf_op jit(solution)/shard_map/ppermute | solution.py:581
  9.9 0.0 collective-permute-start.2
  9.9 0.0 copy-done
  9.9 0.0 copy-done.1
  9.9 0.0 copy-done.2
  9.9 0.0 copy-done.3
  9.9 0.0 copy-done.4
  9.9 0.0 copy-done.5
  9.9 0.0 copy-done.6
  9.9 0.0 copy-start.7
  9.9 0.0 copy-start.8
  9.9 0.0 copy-start.9
  9.9 0.0 copy-start.10
  10.0 0.0 copy-start.11
  10.0 0.0 copy-start.12
  10.0 6.6 %images.2 = (bf16[8,64,128]{2,1,0:T(8,128)(2,1)S(1)}, bf16[8,64,128]{2,1,0:T(8,128)(2,1)S(1)}, f32[2,32,32,128]{3,2,1,0:T(8,128)S(1)}) custom-call(s32[1]{0:T(128)} %bitcast.me, s32[1,1]{1,0:T(1,128)S(6)} %copy.18.valid, f32[64]{0:T(128)S(1)} %copy-done.6, s32[1,1,2,32]{3,2,1,0:T(2,128)S(1)} %bitcast.8, bf16[8,64,1024]{2,1,0:T(8,128)(2,1)S(1)} %bitcast.7, ...), custom_call_target="tpu_custom_call" | custom-call | flops 1310720000 | bytes 1048576 | tf_op jit(solution)/shard_map/images/pallas_call | solution.py:323
  16.6 0.2 collective-permute-start
  16.8 0.0 collective-permute-done.1.refs_2_
  16.8 0.0 collective-permute-done.2.refs_3_
  16.8 1.2 %collective-permute-done.refs_1_ = bf16[8,64,128]{2,1,0:T(8,128)(2,1)S(1)} collective-permute-done((bf16[8,64,128]{2,1,0:T(8,128)(2,1)S(1)}, bf16[8,64,128]{2,1,0:T(8,128)(2,1)S(1)}, u32[]{:S(2)}, u32[]{:S(2)}) %collective-permute-start) | collective-permute-done | bytes 131104 | tf_op jit(solution)/shard_map/ppermute | solution.py:581
  18.0 0.0 copy-done.7
  18.0 0.0 copy-done.8
  18.0 0.0 copy-done.9
  18.0 0.0 copy-done.10
  18.0 0.0 copy-done.11
  18.0 0.0 copy-done.12
  18.0 2.8 %subgrids.1 = bf16[32,136,128]{2,1,0:T(8,128)(2,1)S(1)} custom-call(s32[1]{0:T(128)} %bitcast.me, s32[1,1,1,32]{3,2,1,0:T(1,128)S(1)} %bitcast.9, s32[1,1,1,32]{3,2,1,0:T(1,128)S(1)} %bitcast.10, s32[1,1,1,32]{3,2,1,0:T(1,128)S(1)} %bitcast.11, f32[2,32,32,128]{3,2,1,0:T(8,128)S(1)} %get-tuple-element.24.gain, bf16[256,256]{1,0:T(8,128)(2,1)S(1)} %copy-done.11, ...), custom_call_target="tpu_custom_call" | custom-call | flops 4000000000 | bytes 4194304 | tf_op jit(solution)/shard_map/subgrids/pallas_call | solution.py:405
  20.8 35.1 %all_to_all.5.arrived = bf16[32,136,128]{2,1,0:T(8,128)(2,1)S(1)} all-to-all(bf16[32,136,128]{2,1,0:T(8,128)(2,1)S(1)} %subgrids.1), channel_id=1, replica_groups=mesh['freq'=4,'tile'=8] {'freq','tile'}, dimensions={0} | all-to-all | bytes 2228224 | tf_op jit(solution)/shard_map/all_to_all | solution.py:591
  55.9 0.8 %margin.1 = bf16[8,32,256]{2,1,0:T(8,128)(2,1)S(1)} custom-call(bf16[32,136,128]{2,1,0:T(8,128)(2,1)S(1)} %all_to_all.5.arrived), custom_call_target="tpu_custom_call" | custom-call | tf_op jit(solution)/shard_map/margin/pallas_call | solution.py:481
  56.7 1.1 %collective-permute-start.3 = (bf16[8,32,256]{2,1,0:T(8,128)(2,1)S(1)}, bf16[8,32,256]{2,1,0:T(8,128)(2,1)S(1)}, u32[]{:S(2)}, u32[]{:S(2)}) collective-permute-start(bf16[8,32,256]{2,1,0:T(8,128)(2,1)S(1)} %margin.1), channel_id=1, source_target_pairs={{0,1},{1,2},{2,3},{3,4},{4,5},{5,6},{6,7},{7,8},{8,9},{9,10},{10,1... | collective-permute-start | bytes 393224 | tf_op jit(solution)/shard_map/ppermute | solution.py:594
  57.8 5.4 %tile.1 = (f32[8,256,256]{2,1,0:T(8,128)}, f32[8,32,256]{2,1,0:T(8,128)S(1)}) custom-call(bf16[32,136,128]{2,1,0:T(8,128)(2,1)S(1)} %all_to_all.5.arrived), custom_call_target="tpu_custom_call" | custom-call | flops 4000000000 | bytes 4194304 | tf_op jit(solution)/shard_map/tile/pallas_call | solution.py:543
  63.2 3.0 %collective-permute-done.3 = bf16[8,32,256]{2,1,0:T(8,128)(2,1)S(1)} collective-permute-done((bf16[8,32,256]{2,1,0:T(8,128)(2,1)S(1)}, bf16[8,32,256]{2,1,0:T(8,128)(2,1)S(1)}, u32[]{:S(2)}, u32[]{:S(2)}) %collective-permute-start.3) | collective-permute-done | bytes 131104 | tf_op jit(solution)/shard_map/ppermute | solution.py:594
  66.2 0.7 %add_dynamic-update-slice_fusion = f32[8,256,256]{2,1,0:T(8,128)} fusion(f32[8,256,256]{2,1,0:T(8,128)} %get-tuple-element.29, f32[8,32,256]{2,1,0:T(8,128)S(1)} %get-tuple-element.30, bf16[8,32,256]{2,1,0:T(8,128)(2,1)S(1)} %collective-permute-done.3), kind=kLoop, calls=%fused_computation | loop fusion | flops 131072 | bytes 655360 | tf_op jit(solution)/shard_map/scatter | solution.py:598
Async XLA Ops:
  0.7 9.2 %copy-start = (bf16[1,8,64,1024]{3,2,1,0:T(8,128)(2,1)S(1)}, bf16[1,8,64,1024]{3,2,1,0:T(8,128)(2,1)}, u32[]{:S(2)}) copy-start(bf16[1,8,64,1024]{3,2,1,0:T(8,128)(2,1)} %param.18) | copy-start | bytes 3145732
  0.7 9.2 %copy-start.1 = (bf16[384,512]{1,0:T(8,128)(2,1)S(1)}, bf16[384,512]{1,0:T(8,128)(2,1)}, u32[]{:S(2)}) copy-start(bf16[384,512]{1,0:T(8,128)(2,1)} %constant.43.clone.refs_6_) | copy-start | bytes 1179652
  0.7 9.2 %copy-start.2 = (bf16[512,256]{1,0:T(8,128)(2,1)S(1)}, bf16[512,256]{1,0:T(8,128)(2,1)}, u32[]{:S(2)}) copy-start(bf16[512,256]{1,0:T(8,128)(2,1)} %constant.42.clone.refs_3_.refs_2_) | copy-start | bytes 786436
  0.7 9.2 %copy-start.3 = (f32[32,32]{1,0:T(8,128)S(1)}, f32[32,32]{1,0:T(8,128)}, u32[]{:S(2)}) copy-start(f32[32,32]{1,0:T(8,128)} %refs_5_.1) | copy-start | bytes 12292
  0.7 9.2 %copy-start.4 = (f32[1,2,1024]{2,1,0:T(2,128)S(1)}, f32[1,2,1024]{2,1,0:T(2,128)}, u32[]{:S(2)}) copy-start(f32[1,2,1024]{2,1,0:T(2,128)} %refs_1_.1) | copy-start | bytes 24580
  0.7 9.2 %copy-start.5 = (s32[1,1,32,2]{2,3,1,0:T(2,128)S(1)}, s32[1,1,32,2]{2,3,1,0:T(2,128)}, u32[]{:S(2)}) copy-start(s32[1,1,32,2]{2,3,1,0:T(2,128)} %param.24) | copy-start | bytes 772
  0.7 9.2 %copy-start.6 = (f32[64]{0:T(128)S(1)}, f32[64]{0:T(128)}, u32[]{:S(2)}) copy-start(f32[64]{0:T(128)} %scales.3) | copy-start | bytes 772
  6.9 9.9 %collective-permute-start.1 = (bf16[8,64,128]{2,1,0:T(8,128)(2,1)}, bf16[8,64,128]{2,1,0:T(8,128)(2,1)S(1)}, u32[]{:S(2)}, u32[]{:S(2)}) collective-permute-start(bf16[8,64,128]{2,1,0:T(8,128)(2,1)} %get-tuple-element.27), channel_id=1, source_target_pairs={{0,16},{8,24},{16,0},{24,8},{1,17},{9,25},{17,1},{25,9},{2,18},{10... | collective-permute-start | bytes 393224 | tf_op jit(solution)/shard_map/ppermute | solution.py:581
  9.9 6.9 %collective-permute-start.2 = (bf16[8,64,128]{2,1,0:T(8,128)(2,1)}, bf16[8,64,128]{2,1,0:T(8,128)(2,1)S(1)}, u32[]{:S(2)}, u32[]{:S(2)}) collective-permute-start(bf16[8,64,128]{2,1,0:T(8,128)(2,1)} %get-tuple-element.28), channel_id=1, source_target_pairs={{0,24},{8,16},{16,8},{24,0},{1,25},{9,17},{17,9},{25,1},{2,26},{10... | collective-permute-start | bytes 393224 | tf_op jit(solution)/shard_map/ppermute | solution.py:581
  9.9 8.1 %copy-start.7 = (s32[1,1,32,1]{2,3,1,0:T(1,128)S(1)}, s32[1,1,32,1]{2,3,1,0:T(1,128)}, u32[]{:S(2)}) copy-start(s32[1,1,32,1]{2,3,1,0:T(1,128)} %param.25) | copy-start | bytes 388
  9.9 8.1 %copy-start.8 = (s32[1,1,32,1]{2,3,1,0:T(1,128)S(1)}, s32[1,1,32,1]{2,3,1,0:T(1,128)}, u32[]{:S(2)}) copy-start(s32[1,1,32,1]{2,3,1,0:T(1,128)} %param.26) | copy-start | bytes 388
  9.9 8.1 %copy-start.9 = (s32[1,1,32,1]{2,3,1,0:T(1,128)S(1)}, s32[1,1,32,1]{2,3,1,0:T(1,128)}, u32[]{:S(2)}) copy-start(s32[1,1,32,1]{2,3,1,0:T(1,128)} %param.27) | copy-start | bytes 388
  9.9 8.1 %copy-start.10 = (bf16[256,256]{1,0:T(8,128)(2,1)S(1)}, bf16[256,256]{1,0:T(8,128)(2,1)}, u32[]{:S(2)}) copy-start(bf16[256,256]{1,0:T(8,128)(2,1)} %constant.45.clone.w_low) | copy-start | bytes 393220
  10.0 8.1 %copy-start.11 = (bf16[256,256]{1,0:T(8,128)(2,1)S(1)}, bf16[256,256]{1,0:T(8,128)(2,1)}, u32[]{:S(2)}) copy-start(bf16[256,256]{1,0:T(8,128)(2,1)} %constant.44.clone.w_high) | copy-start | bytes 393220
  10.0 8.1 %copy-start.12 = (bf16[32,192]{1,0:T(8,128)(2,1)S(1)}, bf16[32,192]{1,0:T(8,128)(2,1)}, u32[]{:S(2)}) copy-start(bf16[32,192]{1,0:T(8,128)(2,1)} %constant.46.clone.f_rows) | copy-start | bytes 36868
  16.6 1.4 %collective-permute-start = (bf16[8,64,128]{2,1,0:T(8,128)(2,1)S(1)}, bf16[8,64,128]{2,1,0:T(8,128)(2,1)S(1)}, u32[]{:S(2)}, u32[]{:S(2)}) collective-permute-start(bf16[8,64,128]{2,1,0:T(8,128)(2,1)S(1)} %get-tuple-element.26), channel_id=1, source_target_pairs={{0,8},{8,0},{16,24},{24,16},{1,9},{9,1},{17,25},{25,17},{2,10},{10... | collective-permute-start | bytes 393224 | tf_op jit(solution)/shard_map/ppermute | solution.py:581
  56.7 9.5 %collective-permute-start.3 = (bf16[8,32,256]{2,1,0:T(8,128)(2,1)S(1)}, bf16[8,32,256]{2,1,0:T(8,128)(2,1)S(1)}, u32[]{:S(2)}, u32[]{:S(2)}) collective-permute-start(bf16[8,32,256]{2,1,0:T(8,128)(2,1)S(1)} %margin.1), channel_id=1, source_target_pairs={{0,1},{1,2},{2,3},{3,4},{4,5},{5,6},{6,7},{7,8},{8,9},{9,10},{10,1... | collective-permute-start | bytes 393224 | tf_op jit(solution)/shard_map/ppermute | solution.py:594

commit v6 on v5

--- a/solution.py
+++ b/solution.py
@@ -441,7 +441,7 @@
 
 def margin_kernel(arrived, out_ref, acc, places, chosen, starts):
     sources = arrived.shape[0]
-    batch = 4
+    batch = 8
     first = TILE_W - SG
     acc[...] = jnp.zeros_like(acc)
     places[...] = arrived[:, CAP * 2 * SG :, :].astype(f32)
@@ -486,8 +486,8 @@
         scratch_shapes=[
             pltpu.VMEM((COMPS, BAND_V // LANES, 3 * SG, LANES), f32),
             pltpu.VMEM((arrived.shape[0], POS_ROWS, LANES), f32),
-            pltpu.SMEM((slots + 4,), jnp.int32),
-            pltpu.SMEM((slots + 4,), jnp.int32),
+            pltpu.SMEM((slots + 8,), jnp.int32),
+            pltpu.SMEM((slots + 8,), jnp.int32),
         ],
         compiler_params=pltpu.CompilerParams(vmem_limit_bytes=16 << 20),
         name="margin",

time: 67 us -> 66.9 us (level)
  no operation moved by 1% of the time
where the time goes in v6:
time: 66.9 us; the launch traced here: 66.7 us
  blocking collectives  35.1 us (52%)
  Pallas kernels  21.9 us (33%)
  starting transfers between devices  4.19 us (6%)
  waiting for transfers between devices  3.84 us (6%)
  between operations  0.86 us (1%)
  other arithmetic  0.73 us (1%)
    all_to_all x1, blocking collectives, on_device(): lax.all_to_all(outgoing, ('freq', 'tile'), split_axis=0, concat_axis=0, t...  35.1 us
    pallas_call x2, Pallas kernels, images(): pl.pallas_call(functools.partial(image_kernel, ks, bool(gain_args)), out_...  12.8 us
    pallas_call x1, Pallas kernels, tile_of(): pl.pallas_call(tile_kernel, out_shape=(jax.ShapeDtypeStruct((COMPS, TILE_...  5.43 us
    ppermute x3, starting transfers between devices, make(): part = lax.ppermute(part, 'freq', [(i, i ^ k) for i in range(groups_n)])  3.14 us
    pallas_call x1, Pallas kernels, subgrids(): pl.pallas_call(functools.partial(subgrid_kernel, len(chunks)), out_shape=...  2.77 us
    ppermute x1, waiting for transfers between devices, on_device(): lax.ppermute(margin_of(arrived), ('freq', 'tile'), [(i, (i + 1) % devices...  2.62 us
  transfers between devices with their start and end apart: 4, of which 2 were waited for; matrix products, arithmetic and copies ran while one was open for 0% of the time, Pallas kernels for 18%

profile of v6, /device:TPU:0, one launch (start us, length us, event | category | flops | bytes accessed | tf_op | source)
XLA Modules:
  0.0 66.7 jit_solution(18387546521982441050)
XLA Ops:
  0.7 0.0 copy-start
  0.7 0.0 copy-start.1
  0.7 0.0 copy-start.2
  0.7 0.0 copy-start.3
  0.7 0.0 copy-start.4
  0.7 0.0 copy-start.5
  0.7 0.0 copy-start.6
  0.7 6.2 %images.3 = (bf16[8,64,128]{2,1,0:T(8,128)(2,1)}, bf16[8,64,128]{2,1,0:T(8,128)(2,1)}) custom-call(s32[1]{0:T(128)} %bitcast.me, s32[1,1]{1,0:T(1,128)S(6)} %copy.18.valid, f32[64]{0:T(128)} %scales.3, bf16[8,64,1024]{2,1,0:T(8,128)(2,1)} %bitcast.6, f32[1,2,1024]{2,1,0:T(2,128)} %refs_1_.1, bf16[512,256]{1,0:T(8,128)(2,1)} %constant.42.clone.refs_3_.refs_2_), custom_call_target="tpu_custom_call" | custom-call | flops 1310720000 | bytes 1048576 | tf_op jit(solution)/shard_map/images/pallas_call | solution.py:323
  6.9 2.9 %collective-permute-start.1 = (bf16[8,64,128]{2,1,0:T(8,128)(2,1)}, bf16[8,64,128]{2,1,0:T(8,128)(2,1)S(1)}, u32[]{:S(2)}, u32[]{:S(2)}) collective-permute-start(bf16[8,64,128]{2,1,0:T(8,128)(2,1)} %get-tuple-element.27), channel_id=1, source_target_pairs={{0,16},{8,24},{16,0},{24,8},{1,17},{9,25},{17,1},{25,9},{2,18},{10... | collective-permute-start | bytes 393224 | tf_op jit(solution)/shard_map/ppermute | solution.py:581
  9.9 0.0 collective-permute-start.2
  9.9 0.0 copy-done
  9.9 0.0 copy-done.1
  9.9 0.0 copy-done.2
  9.9 0.0 copy-done.3
  9.9 0.0 copy-done.4
  9.9 0.0 copy-done.5
  9.9 0.0 copy-done.6
  9.9 0.0 copy-start.7
  9.9 0.0 copy-start.8
  9.9 0.0 copy-start.9
  9.9 0.0 copy-start.10
  10.0 0.0 copy-start.11
  10.0 0.0 copy-start.12
  10.0 6.6 %images.2 = (bf16[8,64,128]{2,1,0:T(8,128)(2,1)S(1)}, bf16[8,64,128]{2,1,0:T(8,128)(2,1)S(1)}, f32[2,32,32,128]{3,2,1,0:T(8,128)S(1)}) custom-call(s32[1]{0:T(128)} %bitcast.me, s32[1,1]{1,0:T(1,128)S(6)} %copy.18.valid, f32[64]{0:T(128)S(1)} %copy-done.6, s32[1,1,2,32]{3,2,1,0:T(2,128)S(1)} %bitcast.8, bf16[8,64,1024]{2,1,0:T(8,128)(2,1)S(1)} %bitcast.7, ...), custom_call_target="tpu_custom_call" | custom-call | flops 1310720000 | bytes 1048576 | tf_op jit(solution)/shard_map/images/pallas_call | solution.py:323
  16.6 0.2 collective-permute-start
  16.8 0.0 collective-permute-done.1.refs_2_
  16.8 0.0 collective-permute-done.2.refs_3_
  16.8 1.2 %collective-permute-done.refs_1_ = bf16[8,64,128]{2,1,0:T(8,128)(2,1)S(1)} collective-permute-done((bf16[8,64,128]{2,1,0:T(8,128)(2,1)S(1)}, bf16[8,64,128]{2,1,0:T(8,128)(2,1)S(1)}, u32[]{:S(2)}, u32[]{:S(2)}) %collective-permute-start) | collective-permute-done | bytes 131104 | tf_op jit(solution)/shard_map/ppermute | solution.py:581
  18.0 0.0 copy-done.7
  18.0 0.0 copy-done.8
  18.0 0.0 copy-done.9
  18.0 0.0 copy-done.10
  18.0 0.0 copy-done.11
  18.0 0.0 copy-done.12
  18.0 2.8 %subgrids.1 = bf16[32,136,128]{2,1,0:T(8,128)(2,1)S(1)} custom-call(s32[1]{0:T(128)} %bitcast.me, s32[1,1,1,32]{3,2,1,0:T(1,128)S(1)} %bitcast.9, s32[1,1,1,32]{3,2,1,0:T(1,128)S(1)} %bitcast.10, s32[1,1,1,32]{3,2,1,0:T(1,128)S(1)} %bitcast.11, f32[2,32,32,128]{3,2,1,0:T(8,128)S(1)} %get-tuple-element.24.gain, bf16[256,256]{1,0:T(8,128)(2,1)S(1)} %copy-done.11, ...), custom_call_target="tpu_custom_call" | custom-call | flops 4000000000 | bytes 4194304 | tf_op jit(solution)/shard_map/subgrids/pallas_call | solution.py:405
  20.8 35.1 %all_to_all.5.arrived = bf16[32,136,128]{2,1,0:T(8,128)(2,1)S(1)} all-to-all(bf16[32,136,128]{2,1,0:T(8,128)(2,1)S(1)} %subgrids.1), channel_id=1, replica_groups=mesh['freq'=4,'tile'=8] {'freq','tile'}, dimensions={0} | all-to-all | bytes 2228224 | tf_op jit(solution)/shard_map/all_to_all | solution.py:591
  55.9 0.9 %margin.1 = bf16[8,32,256]{2,1,0:T(8,128)(2,1)S(1)} custom-call(bf16[32,136,128]{2,1,0:T(8,128)(2,1)S(1)} %all_to_all.5.arrived), custom_call_target="tpu_custom_call" | custom-call | tf_op jit(solution)/shard_map/margin/pallas_call | solution.py:481
  56.9 1.1 %collective-permute-start.3 = (bf16[8,32,256]{2,1,0:T(8,128)(2,1)S(1)}, bf16[8,32,256]{2,1,0:T(8,128)(2,1)S(1)}, u32[]{:S(2)}, u32[]{:S(2)}) collective-permute-start(bf16[8,32,256]{2,1,0:T(8,128)(2,1)S(1)} %margin.1), channel_id=1, source_target_pairs={{0,1},{1,2},{2,3},{3,4},{4,5},{5,6},{6,7},{7,8},{8,9},{9,10},{10,1... | collective-permute-start | bytes 393224 | tf_op jit(solution)/shard_map/ppermute | solution.py:594
  57.9 5.4 %tile.1 = (f32[8,256,256]{2,1,0:T(8,128)}, f32[8,32,256]{2,1,0:T(8,128)S(1)}) custom-call(bf16[32,136,128]{2,1,0:T(8,128)(2,1)S(1)} %all_to_all.5.arrived), custom_call_target="tpu_custom_call" | custom-call | flops 4000000000 | bytes 4194304 | tf_op jit(solution)/shard_map/tile/pallas_call | solution.py:543
  63.4 2.6 %collective-permute-done.3 = bf16[8,32,256]{2,1,0:T(8,128)(2,1)S(1)} collective-permute-done((bf16[8,32,256]{2,1,0:T(8,128)(2,1)S(1)}, bf16[8,32,256]{2,1,0:T(8,128)(2,1)S(1)}, u32[]{:S(2)}, u32[]{:S(2)}) %collective-permute-start.3) | collective-permute-done | bytes 131104 | tf_op jit(solution)/shard_map/ppermute | solution.py:594
  66.0 0.7 %add_dynamic-update-slice_fusion = f32[8,256,256]{2,1,0:T(8,128)} fusion(f32[8,256,256]{2,1,0:T(8,128)} %get-tuple-element.29, f32[8,32,256]{2,1,0:T(8,128)S(1)} %get-tuple-element.30, bf16[8,32,256]{2,1,0:T(8,128)(2,1)S(1)} %collective-permute-done.3), kind=kLoop, calls=%fused_computation | loop fusion | flops 131072 | bytes 655360 | tf_op jit(solution)/shard_map/scatter | solution.py:598
Async XLA Ops:
  0.7 9.2 %copy-start = (bf16[1,8,64,1024]{3,2,1,0:T(8,128)(2,1)S(1)}, bf16[1,8,64,1024]{3,2,1,0:T(8,128)(2,1)}, u32[]{:S(2)}) copy-start(bf16[1,8,64,1024]{3,2,1,0:T(8,128)(2,1)} %param.18) | copy-start | bytes 3145732
  0.7 9.2 %copy-start.1 = (bf16[384,512]{1,0:T(8,128)(2,1)S(1)}, bf16[384,512]{1,0:T(8,128)(2,1)}, u32[]{:S(2)}) copy-start(bf16[384,512]{1,0:T(8,128)(2,1)} %constant.43.clone.refs_6_) | copy-start | bytes 1179652
  0.7 9.2 %copy-start.2 = (bf16[512,256]{1,0:T(8,128)(2,1)S(1)}, bf16[512,256]{1,0:T(8,128)(2,1)}, u32[]{:S(2)}) copy-start(bf16[512,256]{1,0:T(8,128)(2,1)} %constant.42.clone.refs_3_.refs_2_) | copy-start | bytes 786436
  0.7 9.2 %copy-start.3 = (f32[32,32]{1,0:T(8,128)S(1)}, f32[32,32]{1,0:T(8,128)}, u32[]{:S(2)}) copy-start(f32[32,32]{1,0:T(8,128)} %refs_5_.1) | copy-start | bytes 12292
  0.7 9.2 %copy-start.4 = (f32[1,2,1024]{2,1,0:T(2,128)S(1)}, f32[1,2,1024]{2,1,0:T(2,128)}, u32[]{:S(2)}) copy-start(f32[1,2,1024]{2,1,0:T(2,128)} %refs_1_.1) | copy-start | bytes 24580
  0.7 9.2 %copy-start.5 = (s32[1,1,32,2]{2,3,1,0:T(2,128)S(1)}, s32[1,1,32,2]{2,3,1,0:T(2,128)}, u32[]{:S(2)}) copy-start(s32[1,1,32,2]{2,3,1,0:T(2,128)} %param.24) | copy-start | bytes 772
  0.7 9.2 %copy-start.6 = (f32[64]{0:T(128)S(1)}, f32[64]{0:T(128)}, u32[]{:S(2)}) copy-start(f32[64]{0:T(128)} %scales.3) | copy-start | bytes 772
  6.9 9.9 %collective-permute-start.1 = (bf16[8,64,128]{2,1,0:T(8,128)(2,1)}, bf16[8,64,128]{2,1,0:T(8,128)(2,1)S(1)}, u32[]{:S(2)}, u32[]{:S(2)}) collective-permute-start(bf16[8,64,128]{2,1,0:T(8,128)(2,1)} %get-tuple-element.27), channel_id=1, source_target_pairs={{0,16},{8,24},{16,0},{24,8},{1,17},{9,25},{17,1},{25,9},{2,18},{10... | collective-permute-start | bytes 393224 | tf_op jit(solution)/shard_map/ppermute | solution.py:581
  9.9 6.9 %collective-permute-start.2 = (bf16[8,64,128]{2,1,0:T(8,128)(2,1)}, bf16[8,64,128]{2,1,0:T(8,128)(2,1)S(1)}, u32[]{:S(2)}, u32[]{:S(2)}) collective-permute-start(bf16[8,64,128]{2,1,0:T(8,128)(2,1)} %get-tuple-element.28), channel_id=1, source_target_pairs={{0,24},{8,16},{16,8},{24,0},{1,25},{9,17},{17,9},{25,1},{2,26},{10... | collective-permute-start | bytes 393224 | tf_op jit(solution)/shard_map/ppermute | solution.py:581
  9.9 8.1 %copy-start.7 = (s32[1,1,32,1]{2,3,1,0:T(1,128)S(1)}, s32[1,1,32,1]{2,3,1,0:T(1,128)}, u32[]{:S(2)}) copy-start(s32[1,1,32,1]{2,3,1,0:T(1,128)} %param.25) | copy-start | bytes 388
  9.9 8.1 %copy-start.8 = (s32[1,1,32,1]{2,3,1,0:T(1,128)S(1)}, s32[1,1,32,1]{2,3,1,0:T(1,128)}, u32[]{:S(2)}) copy-start(s32[1,1,32,1]{2,3,1,0:T(1,128)} %param.26) | copy-start | bytes 388
  9.9 8.1 %copy-start.9 = (s32[1,1,32,1]{2,3,1,0:T(1,128)S(1)}, s32[1,1,32,1]{2,3,1,0:T(1,128)}, u32[]{:S(2)}) copy-start(s32[1,1,32,1]{2,3,1,0:T(1,128)} %param.27) | copy-start | bytes 388
  9.9 8.1 %copy-start.10 = (bf16[256,256]{1,0:T(8,128)(2,1)S(1)}, bf16[256,256]{1,0:T(8,128)(2,1)}, u32[]{:S(2)}) copy-start(bf16[256,256]{1,0:T(8,128)(2,1)} %constant.45.clone.w_low) | copy-start | bytes 393220
  10.0 8.1 %copy-start.11 = (bf16[256,256]{1,0:T(8,128)(2,1)S(1)}, bf16[256,256]{1,0:T(8,128)(2,1)}, u32[]{:S(2)}) copy-start(bf16[256,256]{1,0:T(8,128)(2,1)} %constant.44.clone.w_high) | copy-start | bytes 393220
  10.0 8.1 %copy-start.12 = (bf16[32,192]{1,0:T(8,128)(2,1)S(1)}, bf16[32,192]{1,0:T(8,128)(2,1)}, u32[]{:S(2)}) copy-start(bf16[32,192]{1,0:T(8,128)(2,1)} %constant.46.clone.f_rows) | copy-start | bytes 36868
  16.6 1.4 %collective-permute-start = (bf16[8,64,128]{2,1,0:T(8,128)(2,1)S(1)}, bf16[8,64,128]{2,1,0:T(8,128)(2,1)S(1)}, u32[]{:S(2)}, u32[]{:S(2)}) collective-permute-start(bf16[8,64,128]{2,1,0:T(8,128)(2,1)S(1)} %get-tuple-element.26), channel_id=1, source_target_pairs={{0,8},{8,0},{16,24},{24,16},{1,9},{9,1},{17,25},{25,17},{2,10},{10... | collective-permute-start | bytes 393224 | tf_op jit(solution)/shard_map/ppermute | solution.py:581
  56.9 9.1 %collective-permute-start.3 = (bf16[8,32,256]{2,1,0:T(8,128)(2,1)S(1)}, bf16[8,32,256]{2,1,0:T(8,128)(2,1)S(1)}, u32[]{:S(2)}, u32[]{:S(2)}) collective-permute-start(bf16[8,32,256]{2,1,0:T(8,128)(2,1)S(1)} %margin.1), channel_id=1, source_target_pairs={{0,1},{1,2},{2,3},{3,4},{4,5},{5,6},{6,7},{7,8},{8,9},{9,10},{10,1... | collective-permute-start | bytes 393224 | tf_op jit(solution)/shard_map/ppermute | solution.py:594
